TPU v7x, 512 devices: a whole 4x4x16 slice. The times are simulated.
512 devices in a mesh: arcs: 128 (over x, z, core), coef: 4 (over y).
Axes of the slice: x: 4, y: 4, z: 16, core: 2. Of those that a mesh axis runs over, the one named last changes fastest.
Arguments:
- design: bfloat16 [16384, 9728], P('arcs', 'coef'), as said below
- observed: bfloat16 [16384, 64], P('arcs'), may hold values from -6 to 6
- arc_lengths: int32 [128, 4], P('arcs'), may hold values from 1 to 64, as said below
- arc_months: int32 [128, 4], P('arcs'), may hold values from 0 to 1
- walk_weight: float32 [9728], P('coef'), may hold values from 0.1 to 2
Outputs:
- solution: float32 [9728, 128], P('coef')
Inputs may be any that keep to these rules, and one draw needn't show every extreme that they name: `arc_lengths`: on each index of arcs the arcs fill the first rows one after another; their lengths sum to at most 128 there, and to exactly 128 on some index; no arc is longer than 64 and some arc has exactly that length. `design`: rows and columns have unequal scales.
All inputs are finite; a program needn't handle non-finite values.
Results may differ from a plain program's by a relative error of at most 0.0019.
Values may be sent and summed in bfloat16 or wider, within the bound.
A program may use at most 64 MiB of HBM per device.

v0:
```python
import jax
import jax.numpy as jnp
from jax import lax
from jax.sharding import PartitionSpec as P

NCOEF = 9405
ITERS = 2


epsilon = 1e-06


def fold_months(values, width):
    return values[:width] + values[width:]


def paired(values):
    return jnp.concatenate([values, values])[None, :]


def body(design, observed, arc_lengths, arc_months, walk_weight):
    rows, columns = design.shape
    width = observed.shape[1]
    lengths = arc_lengths[0]
    months = arc_months[0]
    ends = jnp.cumsum(lengths)
    starts = ends - lengths
    positions = jnp.arange(rows, dtype=jnp.int32)
    inside = (positions[None, :] >= starts[:, None]) & (positions[None, :] < ends[:, None])
    month_row = jnp.sum(jnp.where(inside, months[:, None], 0), axis=0)
    is_live = jnp.any(inside, axis=0)
    month_side = (jnp.arange(2 * width, dtype=jnp.int32) >= width).astype(jnp.int32)
    mask_stack = jnp.where(
        is_live[:, None] & (month_row[:, None] == month_side[None, :]), 1.0, 0.0
    ).astype(jnp.float32)
    arcs_count = lax.axis_size("arcs")
    coef_count = lax.axis_size("coef")
    walk_col = walk_weight[:, None]
    offset = lax.axis_index("coef") * columns
    walk_parts = float(arcs_count)
    col_mask = (offset + jnp.arange(columns, dtype=jnp.int32) < NCOEF).astype(jnp.float32)[:, None]

    def adjoint_rows(design_cols, rounded):
        return lax.dot_general(
            design_cols, rounded, (((0,), (0,)), ((), ())), preferred_element_type=jnp.float32
        )

    def adjoint(obs_raw):
        rounded = obs_raw.astype(jnp.bfloat16)
        terms = adjoint_rows(design, rounded)
        total = lax.psum(terms, "arcs")
        return total * col_mask

    def beta_of(obs_raw, walk_raw):
        local = fold_months(jnp.sum(obs_raw * obs_raw, axis=0), width) / float(coef_count)
        local = local + jnp.sum(walk_raw * walk_raw, axis=0) / walk_parts
        return jnp.sqrt(lax.psum(local, ("arcs", "coef")) + epsilon)

    def alpha_of(vec_raw):
        local = fold_months(jnp.sum(vec_raw * vec_raw, axis=0), width)
        total = lax.psum(local, "coef")
        return jnp.sqrt(total + epsilon)

    obs_raw = jnp.concatenate([observed, observed], axis=1).astype(jnp.float32) * mask_stack
    walk_unit = jnp.zeros((columns, width), jnp.float32)
    beta_norm = beta_of(obs_raw, walk_unit)
    vec_raw = adjoint(obs_raw) / paired(beta_norm)
    alpha_norm = alpha_of(vec_raw)
    vec_unit = vec_raw / paired(alpha_norm)
    obs_unit = obs_raw / paired(beta_norm)
    search_dir = vec_unit
    phi_bar = beta_norm
    rho_bar = alpha_norm
    solution = jnp.zeros((columns, 2 * width), jnp.float32)
    for step in range(ITERS):
        forward_rounded = vec_raw.astype(jnp.bfloat16)
        partial_value = jnp.dot(design, forward_rounded, preferred_element_type=jnp.float32)
        obs_raw = (
            lax.psum(partial_value * mask_stack, "coef") / paired(alpha_norm)
            - paired(alpha_norm) * obs_unit
        )
        walk_raw = (
            walk_col * (vec_unit[:, width:] - vec_unit[:, :width]) - alpha_norm[None, :] * walk_unit
        )
        beta_norm = beta_of(obs_raw, walk_raw)
        rho_now = jnp.sqrt(rho_bar * rho_bar + beta_norm * beta_norm)
        rot_cos = rho_bar / rho_now
        rot_sin = beta_norm / rho_now
        phi_step = rot_cos * phi_bar
        phi_bar = rot_sin * phi_bar
        solution = solution + paired(phi_step / rho_now) * search_dir
        if step + 1 < ITERS:
            obs_unit = obs_raw / paired(beta_norm)
            walk_unit = walk_raw / beta_norm[None, :]
            walk_back = jnp.concatenate([-walk_col * walk_unit, walk_col * walk_unit], axis=1)
            vec_raw = (
                adjoint(obs_raw) / paired(beta_norm) + walk_back - paired(beta_norm) * vec_unit
            )
            alpha_norm = alpha_of(vec_raw)
            vec_unit = vec_raw / paired(alpha_norm)
            rho_bar = -rot_cos * alpha_norm
            search_dir = vec_unit - paired(rot_sin * alpha_norm / rho_now) * search_dir
    return solution


def solution(mesh):
    in_specs = (P("arcs", "coef"), P("arcs", None), P("arcs", None), P("arcs", None), P("coef"))
    out_specs = P("coef", None)
    return jax.shard_map(body, mesh=mesh, in_specs=in_specs, out_specs=out_specs, check_vma=False)
```

profile of v0, /device:TPU:1, one launch (start us, length us, event | category | flops | bytes accessed | tf_op | source)
XLA Modules:
  0.0 1051.7 jit_solution(11266106606421155047)
XLA Ops:
  6.5 0.9 reduce-window.7
  7.4 0.7 bitcast_subtract_fusion
  8.1 0.1 fusion.27
  8.2 0.7 select_reduce_fusion
  8.9 2.2 convolution_bitcast_fusion.1
  11.2 0.2 multiply_reduce_fusion.5
  11.5 111.7 %psum.64 = f32[64]{0:T(128)S(1)} all-reduce(f32[64]{0:T(128)S(1)} %add_multiply_fusion), channel_id=1, replica_groups=mesh['arcs'=128,'coef'=4] {'arcs','coef'}, use_global_device_ids=true, to_apply=%region_5.6 | all-reduce | flops 64 | bytes 512 | tf_op jit(solution)/shard_map/psum | solution.py:57
  123.3 234.2 %all-reduce.5.cloned.1.call-done = f32[2432,128]{0,1:T(8,128)} async-done(((f32[2432,128]{0,1:T(8,128)}), f32[2432,128]{0,1:T(8,128)}) %all-reduce.5.cloned.1.call-update) | async-done | bytes 1245200 | tf_op jit(solution)/shard_map/psum | solution.py:51
  357.5 1.7 multiply_reduce_fusion.1
  359.3 8.5 psum.65
  367.9 0.1 pad_maximum_fusion.3
  367.9 1.0 fusion.2
  369.1 0.2 multiply_divide_fusion
  369.3 0.2 multiply_reduce_fusion.2
  369.5 53.6 %all-reduce.7.cloned.1.call-done = f32[128,128]{0,1:T(8,128)} async-done(((f32[128,128]{0,1:T(8,128)}), f32[128,128]{0,1:T(8,128)}) %all-reduce.7.cloned.1.call-update) | async-done | bytes 65552 | tf_op jit(solution)/shard_map/psum | solution.py:79
  423.2 1.0 multiply_reduce_fusion.4
  424.3 106.0 %psum.67 = f32[64]{0:T(128)S(1)} all-reduce(f32[64]{0:T(128)S(1)} %multiply_add_fusion.2), channel_id=1, replica_groups=mesh['arcs'=128,'coef'=4] {'arcs','coef'}, use_global_device_ids=true, to_apply=%region_11.12 | all-reduce | flops 64 | bytes 512 | tf_op jit(solution)/shard_map/psum | solution.py:57
  530.4 1.2 broadcast_multiply_fusion
  531.7 1.4 convolution_bitcast_fusion
  533.1 0.9 broadcast_multiply_fusion.1
  534.0 333.5 %all-reduce.9.cloned.1.call-done = f32[2432,128]{0,1:T(8,128)} async-done(((f32[2432,128]{0,1:T(8,128)}), f32[2432,128]{0,1:T(8,128)}) %all-reduce.9.cloned.1.call-update) | async-done | bytes 1245200 | tf_op jit(solution)/shard_map/psum | solution.py:51
  867.5 2.2 multiply_reduce_fusion
  869.8 8.5 psum.69
  878.4 1.0 fusion.1
  879.4 0.2 broadcast_divide_fusion
  879.6 0.9 copy-done.3
  880.5 0.3 fusion.6
  880.7 52.9 %all-reduce.11.cloned.1.call-done = f32[128,128]{0,1:T(8,128)} async-done(((f32[128,128]{0,1:T(8,128)}), f32[128,128]{0,1:T(8,128)}) %all-reduce.11.cloned.1.call-update) | async-done | bytes 65552 | tf_op jit(solution)/shard_map/psum | solution.py:79
  933.6 1.0 multiply_reduce_fusion.3
  934.7 106.0 %psum.71 = f32[64]{0:T(128)S(1)} all-reduce(f32[64]{0:T(128)S(1)} %multiply_add_fusion.1), channel_id=1, replica_groups=mesh['arcs'=128,'coef'=4] {'arcs','coef'}, use_global_device_ids=true, to_apply=%region_18.19 | all-reduce | flops 64 | bytes 512 | tf_op jit(solution)/shard_map/psum | solution.py:57
  1040.9 1.6 multiply_add_fusion
  1042.4 2.7 copy.7
  (38 shorter events, 1.1 us)
Async XLA Ops:
  6.5 2.4 copy-start
  6.5 351.0 %all-reduce.5.cloned.1.call-start = ((), (), s32[]{:S(2)}) async-start(), calls=%async_computation | async-start | bytes 2490368 | tf_op jit(solution)/shard_map/psum | solution.py:51
  8.9 2.3 copy-start.5
  8.9 2.5 copy-start.4
  11.2 412.0 %all-reduce.7.cloned.1.call-start = ((), (), s32[]{:S(2)}) async-start(), calls=%async_computation.1 | async-start | bytes 131072 | tf_op jit(solution)/shard_map/psum | solution.py:79
  357.5 10.4 copy-start.1
  369.0 498.5 %all-reduce.9.cloned.1.call-start = ((), (), s32[]{:S(2)}) async-start(), calls=%async_computation.2 | async-start | bytes 2490368 | tf_op jit(solution)/shard_map/psum | solution.py:51
  531.7 1.4 copy-start.2
  533.1 400.5 %all-reduce.11.cloned.1.call-start = ((), (), s32[]{:S(2)}) async-start(), calls=%async_computation.3 | async-start | bytes 131072 | tf_op jit(solution)/shard_map/psum | solution.py:79
  879.4 1.1 copy-start.3
Sparse Core Ops, SparseCore 0:
  11.3 346.1 all-reduce.4
  369.1 53.9 all-reduce.6
  533.2 334.2 all-reduce.8
  879.5 54.0 all-reduce.10
where the time goes:
time: 1050 us
  waiting for transfers between devices  674 us (64%)
  blocking collectives  341 us (32%)
  other arithmetic  14 us (1%)
  between operations  13.2 us (1%)
    psum x2, waiting for transfers between devices, adjoint(): total = lax.psum(terms, 'arcs')  568 us
    psum x3, blocking collectives, beta_of(): return jnp.sqrt(lax.psum(local, ('arcs', 'coef')) + epsilon)  324 us
    psum x2, waiting for transfers between devices, body(): lax.psum(partial_value * mask_stack, 'coef') / paired(alpha_norm)  107 us
  transfers between devices with their start and end apart: 4, of which 4 were waited for; matrix products, arithmetic and copies ran while one was open for 0% of the time, Pallas kernels for 0%

commit v1 on v0

v1 whole, which is shorter than its diff:
```python
import functools

import jax
import jax.numpy as jnp
from jax import lax
from jax.experimental import pallas as pl
from jax.experimental.pallas import tpu as pltpu
from jax.sharding import PartitionSpec as P

NCOEF = 9405
EPS = 1e-06
MESH = pl.DeviceIdType.MESH
NX, NZ, NC, NY = 4, 16, 2, 4
TILE = 16
F32, BF16 = jnp.float32, jnp.bfloat16


def kernel(
    design, observed, lengths, months, walk, out,
    d_ref, dt, wt, mask_ref, u_ref, bc_ref,
    cs, cr, xs, xr, tb, zr, own, vh, vl, yb, ny, nc, nx, nz,
    d_sem, cs_s, cs_r, xs_s, xs_r, zs_s, zs_r,
    az_s, az_r, ax_s, ax_r, ac_s, ac_r, y_s, y_r, ny_s, ny_r,
    nc_s, nc_r, nx_s, nx_r, nz_s, nz_r,
):
    rows = d_ref.shape[0]
    columns = d_ref.shape[1]
    tiles = columns // (NC * NX * TILE)
    piece = tiles * TILE
    extras = tiles - NZ
    arc, y = lax.axis_index("arcs"), lax.axis_index("coef")
    core = lax.rem(arc, NC)
    z = lax.rem(arc // NC, NZ)
    x = arc // (NC * NZ)

    def at(x_, z_, c_):
        return ((x_ * NZ + z_) * NC + c_, y)

    def wrap(v, n):
        return lax.rem(v, n)

    sibling = at(x, z, 1 - core)
    hops4 = (2, 1, 3)

    def x_peer(d):
        return wrap(x + d, NX)

    def y_peer(d):
        return (arc, wrap(y + d, NY))

    def extra_owner(e, c_):
        return 5 * e + 3 * c_

    drains = []

    def push(src, dst, ssem, rsem, dev):
        return pltpu.make_async_remote_copy(
            src_ref=src, dst_ref=dst, send_sem=ssem, recv_sem=rsem,
            device_id=dev, device_id_type=MESH,
        )

    def go(copy):
        copy.start()
        drains.append(copy.wait_send)

    def over_z(body):
        def step(d, _):
            body(wrap(z + d, NZ))
            return 0
        lax.fori_loop(1, NZ, step, 0)

    load = pltpu.make_async_copy(design, d_ref, d_sem)
    load.start()

    barrier = pltpu.get_barrier_semaphore()

    def greet(dev):
        pl.semaphore_signal(barrier, inc=1, device_id=dev, device_id_type=MESH)

    greet(sibling)
    for d in hops4:
        greet(at(x_peer(d), z, core))
        greet(y_peer(d))
    over_z(lambda z_: greet(at(x, z_, core)))

    lane = lax.broadcasted_iota(jnp.int32, (rows, 128), 1)
    row = lax.broadcasted_iota(jnp.int32, (rows, 128), 0)
    start = jnp.int32(0)
    month_row = jnp.full((rows, 128), -1, jnp.int32)
    for j in range(lengths.shape[1]):
        end = start + lengths[0, j]
        month_row = jnp.where((row >= start) & (row < end), months[0, j], month_row)
        start = end
    side = (lane >= 64).astype(jnp.int32)
    mask_stack = (month_row == side).astype(F32)
    mask_ref[...] = mask_stack
    half = rows // 2
    low = lax.broadcasted_iota(jnp.int32, (half, 128), 1) < 64
    ob = observed[...].astype(F32)
    ob = jnp.concatenate([ob, ob], axis=1) * mask_stack

    def turn(v):
        return pltpu.roll(v, 64, 1)

    def compact(v):
        s = v + turn(v)
        return jnp.where(low, s[:half], s[half:])

    def expand(v):
        t = turn(v)
        first = jnp.where(low, v, t)
        second = jnp.where(low, t, v)
        return (jnp.concatenate([first, second], axis=0) * mask_ref[...]).astype(BF16)

    def fold(v):
        return v + turn(jnp.broadcast_to(v, (8, 128)))[:1]

    def total(v):
        return jnp.sum(v, axis=0, keepdims=True)

    def padded(parts):
        rest = 4 - len(parts)
        if rest:
            parts = parts + [jnp.zeros((rest, 128), F32)]
        return jnp.concatenate(parts, axis=0)

    bc = compact(ob)
    bc_ref[...] = bc
    u_ref[0] = expand(bc)

    has_extra = jnp.int32(0)
    which = jnp.int32(0)
    for e in range(extras):
        hit = (z == extra_owner(e, core)).astype(jnp.int32)
        has_extra = has_extra + hit
        which = which + e * hit
    base = (core * NX + x) * piece
    tile_of = (z, NZ + which)
    row16 = lax.broadcasted_iota(jnp.int32, (TILE, 128), 0)
    w_parts, keep_parts = [], []
    for s in range(2):
        first = base + tile_of[s] * TILE
        block = first // 128
        inside = first - block * 128
        strip = walk[0:1, pl.ds(pl.multiple_of(block * 128, 128), 128)]
        wt[s] = jnp.broadcast_to(strip, (128, 128)).T
        w_parts.append(wt[s, pl.ds(pl.multiple_of(inside, TILE), TILE), :])
        keep = (y * columns + first + row16) < NCOEF
        if s == 1:
            keep = keep & (jnp.full((TILE, 128), has_extra, jnp.int32) > 0)
        keep_parts.append(keep.astype(F32))
    w_own = jnp.concatenate(w_parts, axis=0)
    keep_own = jnp.concatenate(keep_parts, axis=0)

    load.wait()
    for j in range(columns // 128):
        dt[j * 128:(j + 1) * 128, :] = d_ref[:, j * 128:(j + 1) * 128].T
    pl.semaphore_wait(barrier, 1 + 2 * len(hops4) + NZ - 1)

    def n_core(k, value):
        nc[k, core] = value
        go(push(nc.at[k, core], nc.at[k, core], nc_s.at[k], nc_r.at[k], sibling))

    def n_core_sum(k):
        push(nc.at[k, core], nc.at[k, 1 - core], nc_s.at[k], nc_r.at[k], sibling).wait_recv()
        return nc[k, 0] + nc[k, 1]

    def n_x(k, value):
        nx[k, x] = value
        for d in hops4:
            x_ = x_peer(d)
            go(push(nx.at[k, x], nx.at[k, x], nx_s.at[k, x_], nx_r.at[k, x], at(x_, z, core)))

    def n_x_sum(k):
        for d in hops4:
            x_ = x_peer(d)
            push(nx.at[k, x], nx.at[k, x_], nx_s.at[k, x_], nx_r.at[k, x_], at(x_, z, core)).wait_recv()
        return (nx[k, 0] + nx[k, 1]) + (nx[k, 2] + nx[k, 3])

    def n_z_copy(k, z_):
        return push(nz.at[k, z], nz.at[k, z], nz_s.at[k, z_], nz_r.at[k, z], at(x, z_, core))

    def n_z(k, value):
        nz[k, z] = value
        over_z(lambda z_: n_z_copy(k, z_).start())
        drains.append(lambda: over_z(lambda z_: n_z_copy(k, z_).wait_send()))

    def n_z_sum(k):
        over_z(lambda z_: push(
            nz.at[k, z], nz.at[k, z_], nz_s.at[k, z_], nz_r.at[k, z_], at(x, z_, core)).wait_recv())
        return jnp.sum(nz[k], axis=0)

    def adjoint_piece(r, h, p):
        first = pl.multiple_of((h * NX + p) * piece, TILE)
        value = jnp.dot(dt[pl.ds(first, piece), :], u_ref[r], preferred_element_type=F32)
        return value.reshape(tiles, TILE, 128)

    def reduce_scatter(r, k, norm_value):
        n_core(k, norm_value)
        order = [x_peer(d) for d in hops4] + [x]

        def core_copy(p):
            return push(cs.at[r, p], cr.at[r, p], cs_s.at[r, p], cs_r.at[r, p], sibling)

        for p in order:
            cs[r, p] = adjoint_piece(r, 1 - core, p)
            go(core_copy(p))
        for i, p in enumerate(order):
            mine = adjoint_piece(r, core, p)
            core_copy(p).wait_recv()
            mine = mine + cr[r, p]
            if i < 3:
                xs[r, p] = mine
                go(push(xs.at[r, p], xr.at[r, x], xs_s.at[r, p], xs_r.at[r, x], at(p, z, core)))
            else:
                xr[r, x] = mine
            if i == 0:
                n_x(k, n_core_sum(k))
        for p in order[:3]:
            push(xs.at[r, p], xr.at[r, p], xs_s.at[r, p], xs_r.at[r, p], at(p, z, core)).wait_recv()
        tb[r] = (xr[r, 0] + xr[r, 1]) + (xr[r, 2] + xr[r, 3])

        def main_copy(z_, src):
            return push(tb.at[r, z_], zr.at[r, 0, src], zs_s.at[r, 0, z_], zs_r.at[r, 0, src], at(x, z_, core))

        def extra_copy(e, src):
            z_ = extra_owner(e, core)
            return push(tb.at[r, NZ + e], zr.at[r, 1, src], zs_s.at[r, 1, z_], zs_r.at[r, 1, src], at(x, z_, core))

        over_z(lambda z_: main_copy(z_, z).start())
        for e in range(extras):
            @pl.when(z != extra_owner(e, core))
            def _():
                extra_copy(e, z).start()
        n_z(k, n_x_sum(k))
        zr[r, 0, z] = tb[r, z]
        over_z(lambda z_: main_copy(z_, z_).wait_recv())
        own[r, 0] = jnp.sum(zr[r, 0], axis=0)
        own[r, 1] = jnp.zeros((TILE, 128), F32)

        @pl.when(has_extra > 0)
        def _():
            zr[r, 1, z] = tb[r, NZ + which]
            over_z(lambda z_: push(
                tb.at[r, NZ], zr.at[r, 1, z_], zs_s.at[r, 1, z_], zs_r.at[r, 1, z_], at(x, z_, core)).wait_recv())
            own[r, 1] = jnp.sum(zr[r, 1], axis=0)

        def drain():
            over_z(lambda z_: main_copy(z_, z).wait_send())
            for e in range(extras):
                @pl.when(z != extra_owner(e, core))
                def _():
                    extra_copy(e, z).wait_send()
        drains.append(drain)
        norm = n_z_sum(k)
        return own[r].reshape(2 * TILE, 128) * keep_own, norm

    def gz_main(v, r, q, src, z_):
        ref = v.at[r, core, x, src]
        return push(ref, ref, az_s.at[q, 0, z_], az_r.at[q, 0, src], at(x, z_, core))

    def gz_extra(v, r, q, e, z_):
        ref = v.at[r, core, x, NZ + e]
        return push(ref, ref, az_s.at[q, 1, z_], az_r.at[q, 1, e], at(x, z_, core))

    def gather_z_start(v, r, q, value):
        v[r, core, x, z] = value[:TILE]
        over_z(lambda z_: gz_main(v, r, q, z, z_).start())

        @pl.when(has_extra > 0)
        def _():
            v[r, core, x, NZ + which] = value[TILE:]
            over_z(lambda z_: gz_extra(v, r, q, which, z_).start())

        def drain():
            over_z(lambda z_: gz_main(v, r, q, z, z_).wait_send())

            @pl.when(has_extra > 0)
            def _():
                over_z(lambda z_: gz_extra(v, r, q, which, z_).wait_send())
        drains.append(drain)

    def gather_z_wait(v, r, q):
        over_z(lambda z_: gz_main(v, r, q, z_, z_).wait_recv())
        for e in range(extras):
            @pl.when(z != extra_owner(e, core))
            def _():
                gz_extra(v, r, q, e, extra_owner(e, core)).wait_recv()

    def g_core(v, r, q, c_, p):
        ref = v.at[r, c_, p]
        return push(ref, ref, ac_s.at[q, p], ac_r.at[q, p], sibling)

    def g_x(v, r, q, p, dest):
        ref = v.at[r, core, p]
        return push(ref, ref, ax_s.at[q, dest], ax_r.at[q, p], at(dest, z, core))

    def gather_x_start(v, r, q):
        for d in hops4:
            go(g_x(v, r, q, x, x_peer(d)))
        go(g_core(v, r, q, core, x))

    def gather_x_forward(v, r, q):
        for d in (1, 3, 2):
            p = x_peer(d)
            g_x(v, r, q, p, p).wait_recv()
            go(g_core(v, r, q, core, p))

    def gather_core_wait(v, r, q):
        for d in (0, 1, 3, 2):
            g_core(v, r, q, 1 - core, wrap(x + d, NX)).wait_recv()

    def forward(r):
        value = vh[r].reshape(columns, 128)
        return jnp.dot(d_ref[...], value, preferred_element_type=F32) * mask_ref[...]

    def y_start(r, partial, norms):
        yb[r, y] = partial
        ny[r, y] = norms
        for d in hops4:
            y_ = wrap(y + d, NY)
            go(push(ny.at[r, y], ny.at[r, y], ny_s.at[r, y_], ny_r.at[r, y], y_peer(d)))
            go(push(yb.at[r, y], yb.at[r, y], y_s.at[r, y_], y_r.at[r, y], y_peer(d)))

    def y_wait(r):
        for d in hops4:
            y_ = wrap(y + d, NY)
            push(ny.at[r, y], ny.at[r, y_], ny_s.at[r, y_], ny_r.at[r, y_], y_peer(d)).wait_recv()
            push(yb.at[r, y], yb.at[r, y_], y_s.at[r, y_], y_r.at[r, y_], y_peer(d)).wait_recv()
        return (
            (yb[r, 0] + yb[r, 1]) + (yb[r, 2] + yb[r, 3]),
            (ny[r, 0] + ny[r, 1]) + (ny[r, 2] + ny[r, 3]),
        )

    def split(value):
        hi = value.astype(BF16)
        return hi, (value - hi.astype(F32)).astype(BF16)

    def gather(r, k, value, norms):
        hi, lo = split(value)
        gather_z_start(vh, r, 2 * r, hi)
        n_z(k, norms)
        gather_z_start(vl, r, 2 * r + 1, lo)
        gather_z_wait(vh, r, 2 * r)
        gather_x_start(vh, r, 2 * r)
        n_x(k, n_z_sum(k))
        gather_x_forward(vh, r, 2 * r)
        n_core(k, n_x_sum(k))
        gather_core_wait(vh, r, 2 * r)
        return n_core_sum(k)

    def root(v):
        return jnp.sqrt(v + EPS)

    def walk_of(v):
        return w_own * (turn(v) - v)

    got, norm = reduce_scatter(0, 0, padded([total(bc * bc)]))
    beta1 = root(fold(norm[0:1]))
    v1 = got / beta1
    dv = walk_of(v1)
    dv8 = dv * 0.125
    norms = gather(0, 1, v1, padded([total(v1 * v1), total(dv8 * dv8)]))
    y_start(0, compact(forward(0)), norms)
    gather_z_wait(vl, 0, 1)
    gather_x_start(vl, 0, 1)
    image, norms = y_wait(0)

    alpha1 = root(fold(norms[0:1]))
    o2 = image / alpha1 - alpha1 * (bc_ref[...] / beta1)
    u_ref[1] = expand(o2)
    walk2 = (norms[1:2] / (alpha1 * alpha1)) * 64.0
    got, norm = reduce_scatter(1, 2, padded([total(o2 * o2)]))
    beta2 = jnp.sqrt(fold(norm[0:1]) + walk2 + EPS)
    wz = (dv / alpha1) / beta2
    v2 = got / beta2 - w_own * wz - beta2 * (v1 / alpha1)
    dv8 = walk_of(v2) * 0.125
    norms = gather(
        1, 3, v2,
        padded([total(v2 * v2), total(dv8 * dv8), total(dv8 * wz), total(wz * wz)]),
    )
    y_start(1, compact(forward(1)), norms)
    gather_z_wait(vl, 1, 3)
    gather_x_start(vl, 1, 3)
    gather_x_forward(vl, 0, 1)
    image, norms = y_wait(1)

    alpha2 = root(fold(norms[0:1]))
    o3 = image / alpha2 - alpha2 * (o2 / beta2)
    n_core(4, padded([total(o3 * o3)]))
    square = alpha2 * alpha2
    walk3 = (norms[1:2] / square) * 64.0 - 16.0 * norms[2:3] + square * norms[3:4]
    walk3 = jnp.maximum(walk3, 0.0)
    n_x(4, n_core_sum(4))
    gather_x_forward(vl, 1, 3)
    n_z(4, n_x_sum(4))
    rho1 = jnp.sqrt(alpha1 * alpha1 + beta2 * beta2)
    cos1, sin1 = alpha1 / rho1, beta2 / rho1
    first_step = cos1 * beta1 / rho1
    phi_bar = sin1 * beta1
    rho_bar = -cos1 * alpha2
    theta = sin1 * alpha2 / rho1
    gather_core_wait(vl, 0, 1)
    gather_core_wait(vl, 1, 3)
    beta3 = jnp.sqrt(fold(n_z_sum(4)[0:1]) + walk3 + EPS)
    rho2 = jnp.sqrt(rho_bar * rho_bar + beta3 * beta3)
    second_step = (rho_bar / rho2) * phi_bar / rho2
    weight1 = (first_step - second_step * theta) / alpha1
    weight2 = second_step / alpha2
    for c_ in range(NC):
        for p in range(NX):
            first = (vh[0, c_, p].astype(F32) + vl[0, c_, p].astype(F32)).reshape(piece, 128)
            second = (vh[1, c_, p].astype(F32) + vl[1, c_, p].astype(F32)).reshape(piece, 128)
            begin = (c_ * NX + p) * piece
            out[begin:begin + piece, :] = weight1 * first + weight2 * second

    for drain in drains:
        drain()


def body(design, observed, arc_lengths, arc_months, walk_weight):
    rows, columns = design.shape
    tiles = columns // (NC * NX * TILE)
    vmem = pl.BlockSpec(memory_space=pltpu.VMEM)
    smem = pl.BlockSpec(memory_space=pltpu.SMEM)
    dma = pltpu.SemaphoreType.DMA
    block = (tiles, TILE, 128)
    scratch = [
        pltpu.VMEM((rows, columns), BF16),
        pltpu.VMEM((columns, rows), BF16),
        pltpu.VMEM((2, 128, 128), F32),
        pltpu.VMEM((rows, 128), F32),
        pltpu.VMEM((2, rows, 128), BF16),
        pltpu.VMEM((rows // 2, 128), F32),
        pltpu.VMEM((2, NX) + block, F32),
        pltpu.VMEM((2, NX) + block, F32),
        pltpu.VMEM((2, NX) + block, F32),
        pltpu.VMEM((2, NX) + block, F32),
        pltpu.VMEM((2,) + block, F32),
        pltpu.VMEM((2, 2, NZ, TILE, 128), F32),
        pltpu.VMEM((2, 2, TILE, 128), F32),
        pltpu.VMEM((2, NC, NX) + block, BF16),
        pltpu.VMEM((2, NC, NX) + block, BF16),
        pltpu.VMEM((2, NY, rows // 2, 128), F32),
        pltpu.VMEM((2, NY, 4, 128), F32),
        pltpu.VMEM((5, NC, 4, 128), F32),
        pltpu.VMEM((5, NX, 4, 128), F32),
        pltpu.VMEM((5, NZ, 4, 128), F32),
        dma,
        dma((2, NX)), dma((2, NX)),
        dma((2, NX)), dma((2, NX)),
        dma((2, 2, NZ)), dma((2, 2, NZ)),
        dma((4, 2, NZ)), dma((4, 2, NZ)),
        dma((4, NX)), dma((4, NX)),
        dma((4, NX)), dma((4, NX)),
        dma((2, NY)), dma((2, NY)),
        dma((2, NY)), dma((2, NY)),
        dma((5,)), dma((5,)),
        dma((5, NX)), dma((5, NX)),
        dma((5, NZ)), dma((5, NZ)),
    ]
    return pl.pallas_call(
        kernel,
        out_shape=jax.ShapeDtypeStruct((columns, 128), F32),
        in_specs=[pl.BlockSpec(memory_space=pl.ANY), vmem, smem, smem, vmem],
        out_specs=vmem,
        scratch_shapes=scratch,
        compiler_params=pltpu.CompilerParams(
            collective_id=0, has_side_effects=True, vmem_limit_bytes=40 * 1024 * 1024
        ),
    )(design, observed, arc_lengths, arc_months, walk_weight.reshape(1, columns))


def solution(mesh):
    in_specs = (P("arcs", "coef"), P("arcs", None), P("arcs", None), P("arcs", None), P("coef"))
    return jax.shard_map(
        body, mesh=mesh, in_specs=in_specs, out_specs=P("coef", None), check_vma=False
    )
```

time: 1050 us -> 132 us (0.13)
  waiting for transfers between devices: 674 us -> 0 us
  blocking collectives: 341 us -> 0 us
  Pallas kernels: 0 us -> 127 us
  other arithmetic: 14 us -> 0 us
  between operations: 13.2 us -> 0.02 us
    psum x4 -> x0, waiting for transfers between devices: 674 us -> none  [the longest x2 568 us: adjoint(): total = lax.psum(terms, 'arcs')]
    psum x5 -> x0, blocking collectives: 341 us -> none  [the longest x3 324 us: beta_of(): return jnp.sqrt(lax.psum(local, ('arcs', 'coef')) + epsilon)]
    pallas_call x0 -> x1, Pallas kernels: none -> 127 us  [body(): pl.pallas_call(kernel, out_shape=jax.ShapeDtypeStruct((columns, 128), F32...]
  transfers between devices with their start and end apart: 4 -> 0, of which waited for: 4 -> 0; matrix products, arithmetic and copies ran while one was open for 0% -> 0% of each run, Pallas kernels for 0% -> 0%
where the time goes in v1:
time: 132 us
  Pallas kernels  127 us (96%)
  local copies, waits for them, and re-layouts  4.96 us (4%)
    pallas_call x1, Pallas kernels, body(): pl.pallas_call(kernel, out_shape=jax.ShapeDtypeStruct((columns, 128), F32...  127 us
    unnamed x8, local copies, waits for them, and re-layouts  4.25 us

profile of v1, /device:TPU:1, one launch (start us, length us, event | category | flops | bytes accessed | tf_op | source)
XLA Modules:
  0.0 131.8 jit_solution(12406069864986845629)
XLA Ops:
  0.0 0.7 reshape.3.walk
  0.7 0.8 copy.6.observed
  1.5 0.0 copy-start
  1.6 1.1 copy-done
  2.6 0.0 copy-start.1
  2.6 0.7 copy-done.1
  3.3 0.0 copy-start.2
  3.3 0.7 copy-done.2
  3.9 126.8 %shard_map.55 = f32[2432,128]{1,0:T(8,128)S(1)} custom-call(bf16[128,2432]{1,0:T(8,128)(2,1)S(1)} %copy-done, bf16[128,64]{1,0:T(8,128)(2,1)S(1)} %copy.6.observed, s32[1,4]{1,0:T(1,128)S(1)} %copy-done.1, s32[1,4]{1,0:T(1,128)S(1)} %copy-done.2, f32[1,2432]{1,0:T(1,128)S(1)} %reshape.3.walk), custom_call_target="tpu_custom_call" | custom-call | tf_op jit(solution)/shard_map/pallas_call | solution.py:462
  130.8 1.0 copy.8
Async XLA Ops:
  1.5 1.1 copy-start
  2.6 0.7 copy-start.1
  3.3 0.7 copy-start.2

commit v2 on v1

--- a/solution.py
+++ b/solution.py
@@ -17,9 +17,9 @@
 
 def kernel(
     design, observed, lengths, months, walk, out,
-    d_ref, dt, wt, mask_ref, u_ref, bc_ref,
+    d_ref, dt, ob_ref, len_ref, mon_ref, walk_ref, wt, mask_ref, u_ref, bc_ref,
     cs, cr, xs, xr, tb, zr, own, vh, vl, yb, ny, nc, nx, nz,
-    d_sem, cs_s, cs_r, xs_s, xs_r, zs_s, zs_r,
+    in_sem, cs_s, cs_r, xs_s, xs_r, zs_s, zs_r,
     az_s, az_r, ax_s, ax_r, ac_s, ac_r, y_s, y_r, ny_s, ny_r,
     nc_s, nc_r, nx_s, nx_r, nz_s, nz_r,
 ):
@@ -64,69 +64,22 @@
         drains.append(copy.wait_send)
 
     def over_z(body):
-        def step(d, _):
-            body(wrap(z + d, NZ))
+        def step(i, _):
+            away = lax.div(i + 1, 2) * (1 - 2 * lax.rem(i, 2))
+            body(wrap(z + NZ // 2 + away, NZ))
             return 0
-        lax.fori_loop(1, NZ, step, 0)
-
-    load = pltpu.make_async_copy(design, d_ref, d_sem)
-    load.start()
+        lax.fori_loop(0, NZ - 1, step, 0)
 
     barrier = pltpu.get_barrier_semaphore()
 
     def greet(dev):
         pl.semaphore_signal(barrier, inc=1, device_id=dev, device_id_type=MESH)
 
-    greet(sibling)
+    over_z(lambda z_: greet(at(x, z_, core)))
     for d in hops4:
         greet(at(x_peer(d), z, core))
         greet(y_peer(d))
-    over_z(lambda z_: greet(at(x, z_, core)))
-
-    lane = lax.broadcasted_iota(jnp.int32, (rows, 128), 1)
-    row = lax.broadcasted_iota(jnp.int32, (rows, 128), 0)
-    start = jnp.int32(0)
-    month_row = jnp.full((rows, 128), -1, jnp.int32)
-    for j in range(lengths.shape[1]):
-        end = start + lengths[0, j]
-        month_row = jnp.where((row >= start) & (row < end), months[0, j], month_row)
-        start = end
-    side = (lane >= 64).astype(jnp.int32)
-    mask_stack = (month_row == side).astype(F32)
-    mask_ref[...] = mask_stack
-    half = rows // 2
-    low = lax.broadcasted_iota(jnp.int32, (half, 128), 1) < 64
-    ob = observed[...].astype(F32)
-    ob = jnp.concatenate([ob, ob], axis=1) * mask_stack
-
-    def turn(v):
-        return pltpu.roll(v, 64, 1)
-
-    def compact(v):
-        s = v + turn(v)
-        return jnp.where(low, s[:half], s[half:])
-
-    def expand(v):
-        t = turn(v)
-        first = jnp.where(low, v, t)
-        second = jnp.where(low, t, v)
-        return (jnp.concatenate([first, second], axis=0) * mask_ref[...]).astype(BF16)
-
-    def fold(v):
-        return v + turn(jnp.broadcast_to(v, (8, 128)))[:1]
-
-    def total(v):
-        return jnp.sum(v, axis=0, keepdims=True)
-
-    def padded(parts):
-        rest = 4 - len(parts)
-        if rest:
-            parts = parts + [jnp.zeros((rest, 128), F32)]
-        return jnp.concatenate(parts, axis=0)
-
-    bc = compact(ob)
-    bc_ref[...] = bc
-    u_ref[0] = expand(bc)
+    greet(sibling)
 
     has_extra = jnp.int32(0)
     which = jnp.int32(0)
@@ -135,15 +88,75 @@
         has_extra = has_extra + hit
         which = which + e * hit
     base = (core * NX + x) * piece
-    tile_of = (z, NZ + which)
+    firsts = [base + z * TILE, base + (NZ + which) * TILE]
+
+    loads = [
+        pltpu.make_async_copy(src, dst, in_sem.at[i])
+        for i, (src, dst) in enumerate([
+            (lengths, len_ref), (months, mon_ref), (observed, ob_ref), (design, d_ref),
+        ] + [
+            (walk.at[pl.ds(pl.multiple_of(f // 128 * 128, 128), 128)], walk_ref.at[s])
+            for s, f in enumerate(firsts)
+        ])
+    ]
+    for load in loads:
+        load.start()
+
+    lane = lax.broadcasted_iota(jnp.int32, (rows, 128), 1)
+    row = lax.broadcasted_iota(jnp.int32, (rows, 128), 0)
+    start = jnp.int32(0)
+    month_row = jnp.full((rows, 128), -1, jnp.int32)
+    loads[0].wait()
+    loads[1].wait()
+    for j in range(len_ref.shape[1]):
+        end = start + len_ref[0, j]
+        month_row = jnp.where((row >= start) & (row < end), mon_ref[0, j], month_row)
+        start = end
+    side = (lane >= 64).astype(jnp.int32)
+    mask_stack = (month_row == side).astype(F32)
+    mask_ref[...] = mask_stack
+    half = rows // 2
+    low = lax.broadcasted_iota(jnp.int32, (half, 128), 1) < 64
+    loads[2].wait()
+    ob = ob_ref[...].astype(F32)
+    ob = jnp.concatenate([ob, ob], axis=0).T * mask_stack
+
+    def turn(v):
+        return pltpu.roll(v, 64, 1)
+
+    def compact(v):
+        s = v + turn(v)
+        return jnp.where(low, s[:half], s[half:])
+
+    def expand(v):
+        t = turn(v)
+        first = jnp.where(low, v, t)
+        second = jnp.where(low, t, v)
+        return (jnp.concatenate([first, second], axis=0) * mask_ref[...]).astype(BF16)
+
+    def fold(v):
+        return v + turn(jnp.broadcast_to(v, (8, 128)))[:1]
+
+    def total(v):
+        return jnp.sum(v, axis=0, keepdims=True)
+
+    def padded(parts):
+        rest = 4 - len(parts)
+        if rest:
+            parts = parts + [jnp.zeros((rest, 128), F32)]
+        return jnp.concatenate(parts, axis=0)
+
+    bc = compact(ob)
+    bc_ref[...] = bc
+    u_ref[0] = expand(bc)
+
     row16 = lax.broadcasted_iota(jnp.int32, (TILE, 128), 0)
     w_parts, keep_parts = [], []
     for s in range(2):
-        first = base + tile_of[s] * TILE
-        block = first // 128
-        inside = first - block * 128
-        strip = walk[0:1, pl.ds(pl.multiple_of(block * 128, 128), 128)]
-        wt[s] = jnp.broadcast_to(strip, (128, 128)).T
+        first = firsts[s]
+        inside = lax.rem(first, 128)
+        loads[4 + s].wait()
+        wt[s] = jnp.broadcast_to(walk_ref[s:s + 1, :], (128, 128)).T
         w_parts.append(wt[s, pl.ds(pl.multiple_of(inside, TILE), TILE), :])
         keep = (y * columns + first + row16) < NCOEF
         if s == 1:
@@ -152,7 +165,7 @@
     w_own = jnp.concatenate(w_parts, axis=0)
     keep_own = jnp.concatenate(keep_parts, axis=0)
 
-    load.wait()
+    loads[3].wait()
     for j in range(columns // 128):
         dt[j * 128:(j + 1) * 128, :] = d_ref[:, j * 128:(j + 1) * 128].T
     pl.semaphore_wait(barrier, 1 + 2 * len(hops4) + NZ - 1)
@@ -216,6 +229,7 @@
                 xr[r, x] = mine
             if i == 0:
                 n_x(k, n_core_sum(k))
+        n_z(k, n_x_sum(k))
         for p in order[:3]:
             push(xs.at[r, p], xr.at[r, p], xs_s.at[r, p], xs_r.at[r, p], at(p, z, core)).wait_recv()
         tb[r] = (xr[r, 0] + xr[r, 1]) + (xr[r, 2] + xr[r, 3])
@@ -227,12 +241,11 @@
             z_ = extra_owner(e, core)
             return push(tb.at[r, NZ + e], zr.at[r, 1, src], zs_s.at[r, 1, z_], zs_r.at[r, 1, src], at(x, z_, core))
 
-        over_z(lambda z_: main_copy(z_, z).start())
         for e in range(extras):
             @pl.when(z != extra_owner(e, core))
             def _():
                 extra_copy(e, z).start()
-        n_z(k, n_x_sum(k))
+        over_z(lambda z_: main_copy(z_, z).start())
         zr[r, 0, z] = tb[r, z]
         over_z(lambda z_: main_copy(z_, z_).wait_recv())
         own[r, 0] = jnp.sum(zr[r, 0], axis=0)
@@ -422,12 +435,16 @@
     rows, columns = design.shape
     tiles = columns // (NC * NX * TILE)
     vmem = pl.BlockSpec(memory_space=pltpu.VMEM)
-    smem = pl.BlockSpec(memory_space=pltpu.SMEM)
+    hbm = pl.BlockSpec(memory_space=pltpu.HBM)
     dma = pltpu.SemaphoreType.DMA
     block = (tiles, TILE, 128)
     scratch = [
         pltpu.VMEM((rows, columns), BF16),
         pltpu.VMEM((columns, rows), BF16),
+        pltpu.VMEM((observed.shape[1], rows), BF16),
+        pltpu.SMEM(arc_lengths.shape, jnp.int32),
+        pltpu.SMEM(arc_months.shape, jnp.int32),
+        pltpu.VMEM((2, 128), F32),
         pltpu.VMEM((2, 128, 128), F32),
         pltpu.VMEM((rows, 128), F32),
         pltpu.VMEM((2, rows, 128), BF16),
@@ -446,7 +463,7 @@
         pltpu.VMEM((5, NC, 4, 128), F32),
         pltpu.VMEM((5, NX, 4, 128), F32),
         pltpu.VMEM((5, NZ, 4, 128), F32),
-        dma,
+        dma((6,)),
         dma((2, NX)), dma((2, NX)),
         dma((2, NX)), dma((2, NX)),
         dma((2, 2, NZ)), dma((2, 2, NZ)),
@@ -462,13 +479,13 @@
     return pl.pallas_call(
         kernel,
         out_shape=jax.ShapeDtypeStruct((columns, 128), F32),
-        in_specs=[pl.BlockSpec(memory_space=pl.ANY), vmem, smem, smem, vmem],
+        in_specs=[hbm] * 5,
         out_specs=vmem,
         scratch_shapes=scratch,
         compiler_params=pltpu.CompilerParams(
-            collective_id=0, has_side_effects=True, vmem_limit_bytes=40 * 1024 * 1024
+            collective_id=0, has_side_effects=True, vmem_limit_bytes=63 * 1024 * 1024
         ),
-    )(design, observed, arc_lengths, arc_months, walk_weight.reshape(1, columns))
+    )(design, observed.T, arc_lengths, arc_months, walk_weight)
 
 
 def solution(mesh):

time: 132 us -> 123 us (0.932)
  Pallas kernels: 127 us -> 120 us
  local copies, waits for them, and re-layouts: 4.96 us -> 2.41 us
    pallas_call x1, Pallas kernels: 127 us -> 120 us  [body(): pl.pallas_call(kernel, out_shape=jax.ShapeDtypeStruct((columns, 128), F32...]
    unnamed x8 -> x1, local copies, waits for them, and re-layouts: 4.25 us -> 2.41 us
where the time goes in v2:
time: 123 us; the launch traced here: 122 us
  Pallas kernels  120 us (98%)
  local copies, waits for them, and re-layouts  2.41 us (2%)
    pallas_call x1, Pallas kernels, body(): pl.pallas_call(kernel, out_shape=jax.ShapeDtypeStruct((columns, 128), F32...  120 us

profile of v2, /device:TPU:1, one launch (start us, length us, event | category | flops | bytes accessed | tf_op | source)
XLA Modules:
  0.0 121.9 jit_solution(9287367923291250603)
XLA Ops:
  0.0 119.5 %shard_map.55 = f32[2432,128]{1,0:T(8,128)} custom-call(bf16[128,2432]{1,0:T(8,128)(2,1)} %design.1, bf16[64,128]{1,0:T(8,128)(2,1)} %bitcast.1, s32[1,4]{1,0:T(1,128)} %lengths.1, s32[1,4]{1,0:T(1,128)} %months.1, f32[2432]{0:T(1024)} %walk.1), custom_call_target="tpu_custom_call" | custom-call | tf_op jit(solution)/shard_map/pallas_call | solution.py:479
  119.5 2.4 %copy.7 = f32[2432,128]{1,0:T(8,128)} copy(f32[2432,128]{1,0:T(8,128)} %shard_map.55) | data formatting | bytes 2490368

commit v3 on v2

--- a/solution.py
+++ b/solution.py
@@ -18,9 +18,9 @@
 def kernel(
     design, observed, lengths, months, walk, out,
     d_ref, dt, ob_ref, len_ref, mon_ref, walk_ref, wt, mask_ref, u_ref, bc_ref,
-    cs, cr, xs, xr, tb, zr, own, vh, vl, yb, ny, nc, nx, nz,
-    in_sem, cs_s, cs_r, xs_s, xs_r, zs_s, zs_r,
-    az_s, az_r, ax_s, ax_r, ac_s, ac_r, y_s, y_r, ny_s, ny_r,
+    cs, cr, xs, xr, tb, zr, own, vh, vl, yb, nc, nx, nz,
+    in_sem, cs_s, cs_r, xs_s, xs_r, zs_s, zs_r, ze_s, ze_r,
+    az_s, az_r, ae_s, ae_r, ax_s, ax_r, ac_s, ac_r, y_s, y_r,
     nc_s, nc_r, nx_s, nx_r, nz_s, nz_r,
 ):
     rows = d_ref.shape[0]
@@ -59,16 +59,26 @@
             device_id=dev, device_id_type=MESH,
         )
 
-    def go(copy):
-        copy.start()
-        drains.append(copy.wait_send)
+    def sent(ref, sem):
+        drains.append(push(ref, ref, sem, sem, sibling).wait_send)
+
+    def received(ref, sem):
+        push(ref, ref, sem, sem, sibling).wait_recv()
+
+    def nth(i, middle):
+        return middle + lax.div(i + 1, 2) * (1 - 2 * lax.rem(i, 2))
+
+    def loop(count, body):
+        def step(i, _):
+            body(i)
+            return 0
+        lax.fori_loop(0, count, step, 0)
 
     def over_z(body):
-        def step(i, _):
-            away = lax.div(i + 1, 2) * (1 - 2 * lax.rem(i, 2))
-            body(wrap(z + NZ // 2 + away, NZ))
-            return 0
-        lax.fori_loop(0, NZ - 1, step, 0)
+        loop(NZ - 1, lambda i: body(wrap(z + nth(i, NZ // 2), NZ)))
+
+    def over_x(body):
+        loop(NX - 1, lambda i: body(wrap(x + nth(i, NX // 2), NX)))
 
     barrier = pltpu.get_barrier_semaphore()
 
@@ -172,35 +182,29 @@
 
     def n_core(k, value):
         nc[k, core] = value
-        go(push(nc.at[k, core], nc.at[k, core], nc_s.at[k], nc_r.at[k], sibling))
+        push(nc.at[k, core], nc.at[k, core], nc_s.at[k], nc_r.at[k], sibling).start()
+        sent(nc.at[k, 0], nc_s.at[k])
 
     def n_core_sum(k):
-        push(nc.at[k, core], nc.at[k, 1 - core], nc_s.at[k], nc_r.at[k], sibling).wait_recv()
+        received(nc.at[k, 0], nc_r.at[k])
         return nc[k, 0] + nc[k, 1]
 
     def n_x(k, value):
         nx[k, x] = value
-        for d in hops4:
-            x_ = x_peer(d)
-            go(push(nx.at[k, x], nx.at[k, x], nx_s.at[k, x_], nx_r.at[k, x], at(x_, z, core)))
+        over_x(lambda x_: push(nx.at[k, x], nx.at[k, x], nx_s.at[k], nx_r.at[k], at(x_, z, core)).start())
+        sent(nx.at[k, pl.ds(0, NX - 1)], nx_s.at[k])
 
     def n_x_sum(k):
-        for d in hops4:
-            x_ = x_peer(d)
-            push(nx.at[k, x], nx.at[k, x_], nx_s.at[k, x_], nx_r.at[k, x_], at(x_, z, core)).wait_recv()
+        received(nx.at[k, pl.ds(0, NX - 1)], nx_r.at[k])
         return (nx[k, 0] + nx[k, 1]) + (nx[k, 2] + nx[k, 3])
-
-    def n_z_copy(k, z_):
-        return push(nz.at[k, z], nz.at[k, z], nz_s.at[k, z_], nz_r.at[k, z], at(x, z_, core))
 
     def n_z(k, value):
         nz[k, z] = value
-        over_z(lambda z_: n_z_copy(k, z_).start())
-        drains.append(lambda: over_z(lambda z_: n_z_copy(k, z_).wait_send()))
+        over_z(lambda z_: push(nz.at[k, z], nz.at[k, z], nz_s.at[k], nz_r.at[k], at(x, z_, core)).start())
+        sent(nz.at[k, pl.ds(0, NZ - 1)], nz_s.at[k])
 
     def n_z_sum(k):
-        over_z(lambda z_: push(
-            nz.at[k, z], nz.at[k, z_], nz_s.at[k, z_], nz_r.at[k, z_], at(x, z_, core)).wait_recv())
+        received(nz.at[k, pl.ds(0, NZ - 1)], nz_r.at[k])
         return jnp.sum(nz[k], axis=0)
 
     def adjoint_piece(r, h, p):
@@ -210,140 +214,120 @@
 
     def reduce_scatter(r, k, norm_value):
         n_core(k, norm_value)
-        order = [x_peer(d) for d in hops4] + [x]
-
-        def core_copy(p):
-            return push(cs.at[r, p], cr.at[r, p], cs_s.at[r, p], cs_r.at[r, p], sibling)
-
-        for p in order:
+
+        def theirs(i):
+            p = wrap(x + nth(i, NX // 2), NX)
             cs[r, p] = adjoint_piece(r, 1 - core, p)
-            go(core_copy(p))
-        for i, p in enumerate(order):
-            mine = adjoint_piece(r, core, p)
-            core_copy(p).wait_recv()
-            mine = mine + cr[r, p]
-            if i < 3:
-                xs[r, p] = mine
-                go(push(xs.at[r, p], xr.at[r, x], xs_s.at[r, p], xs_r.at[r, x], at(p, z, core)))
-            else:
-                xr[r, x] = mine
-            if i == 0:
-                n_x(k, n_core_sum(k))
+            push(cs.at[r, p], cr.at[r, p], cs_s.at[r], cs_r.at[r, p], sibling).start()
+        loop(NX, theirs)
+        sent(cs.at[r], cs_s.at[r])
+
+        def mine(p):
+            value = adjoint_piece(r, core, p)
+            received(cr.at[r, p], cs_r.at[r, p])
+            return value + cr[r, p]
+
+        def away(p):
+            xs[r, p] = mine(p)
+            push(xs.at[r, p], xr.at[r, x], xs_s.at[r], xs_r.at[r], at(p, z, core)).start()
+        over_x(away)
+        sent(xs.at[r, pl.ds(0, NX - 1)], xs_s.at[r])
+        n_x(k, n_core_sum(k))
+        xr[r, x] = mine(x)
         n_z(k, n_x_sum(k))
-        for p in order[:3]:
-            push(xs.at[r, p], xr.at[r, p], xs_s.at[r, p], xs_r.at[r, p], at(p, z, core)).wait_recv()
+        received(xr.at[r, pl.ds(0, NX - 1)], xs_r.at[r])
         tb[r] = (xr[r, 0] + xr[r, 1]) + (xr[r, 2] + xr[r, 3])
 
-        def main_copy(z_, src):
-            return push(tb.at[r, z_], zr.at[r, 0, src], zs_s.at[r, 0, z_], zs_r.at[r, 0, src], at(x, z_, core))
-
-        def extra_copy(e, src):
-            z_ = extra_owner(e, core)
-            return push(tb.at[r, NZ + e], zr.at[r, 1, src], zs_s.at[r, 1, z_], zs_r.at[r, 1, src], at(x, z_, core))
-
+        def elsewhere(e, act):
+            pl.when(z != extra_owner(e, core))(act)
+
+        for e in range(extras):
+            elsewhere(e, lambda e=e: push(
+                tb.at[r, NZ + e], zr.at[r, 1, z], ze_s.at[r, e], ze_r.at[r],
+                at(x, extra_owner(e, core), core)).start())
+        over_z(lambda z_: push(
+            tb.at[r, z_], zr.at[r, 0, z], zs_s.at[r], zs_r.at[r], at(x, z_, core)).start())
+        sent(tb.at[r, pl.ds(0, NZ - 1)], zs_s.at[r])
+        zr[r, 0, z] = tb[r, z]
+        own[r, 1] = jnp.zeros((TILE, 128), F32)
+
+        @pl.when(has_extra > 0)
+        def _():
+            zr[r, 1, z] = tb[r, NZ + which]
+            received(zr.at[r, 1, pl.ds(0, NZ - 1)], ze_r.at[r])
+            own[r, 1] = jnp.sum(zr[r, 1], axis=0)
+        norm = n_z_sum(k)
+        received(zr.at[r, 0, pl.ds(0, NZ - 1)], zs_r.at[r])
+        own[r, 0] = jnp.sum(zr[r, 0], axis=0)
+
+        def drain():
+            for e in range(extras):
+                elsewhere(e, lambda e=e: push(
+                    tb.at[r, 0], tb.at[r, 0], ze_s.at[r, e], ze_s.at[r, e], sibling).wait_send())
+        drains.append(drain)
+        return own[r].reshape(2 * TILE, 128) * keep_own, norm
+
+    def gather_z_start(v, r, q, value):
+        @pl.when(has_extra > 0)
+        def _():
+            ref = v.at[r, core, x, NZ + which]
+            v[r, core, x, NZ + which] = value[TILE:]
+            over_z(lambda z_: push(ref, ref, ae_s.at[q], ae_r.at[q, which], at(x, z_, core)).start())
+
+        main = v.at[r, core, x, z]
+        v[r, core, x, z] = value[:TILE]
+        over_z(lambda z_: push(main, main, az_s.at[q], az_r.at[q], at(x, z_, core)).start())
+        many = v.at[r, core, x, pl.ds(0, NZ - 1)]
+        sent(many, az_s.at[q])
+
+        def drain():
+            @pl.when(has_extra > 0)
+            def _():
+                push(many, many, ae_s.at[q], ae_s.at[q], sibling).wait_send()
+        drains.append(drain)
+
+    def gather_z_wait(v, r, q):
+        received(v.at[r, core, x, pl.ds(0, NZ - 1)], az_r.at[q])
         for e in range(extras):
             @pl.when(z != extra_owner(e, core))
             def _():
-                extra_copy(e, z).start()
-        over_z(lambda z_: main_copy(z_, z).start())
-        zr[r, 0, z] = tb[r, z]
-        over_z(lambda z_: main_copy(z_, z_).wait_recv())
-        own[r, 0] = jnp.sum(zr[r, 0], axis=0)
-        own[r, 1] = jnp.zeros((TILE, 128), F32)
-
-        @pl.when(has_extra > 0)
-        def _():
-            zr[r, 1, z] = tb[r, NZ + which]
-            over_z(lambda z_: push(
-                tb.at[r, NZ], zr.at[r, 1, z_], zs_s.at[r, 1, z_], zs_r.at[r, 1, z_], at(x, z_, core)).wait_recv())
-            own[r, 1] = jnp.sum(zr[r, 1], axis=0)
-
-        def drain():
-            over_z(lambda z_: main_copy(z_, z).wait_send())
-            for e in range(extras):
-                @pl.when(z != extra_owner(e, core))
-                def _():
-                    extra_copy(e, z).wait_send()
-        drains.append(drain)
-        norm = n_z_sum(k)
-        return own[r].reshape(2 * TILE, 128) * keep_own, norm
-
-    def gz_main(v, r, q, src, z_):
-        ref = v.at[r, core, x, src]
-        return push(ref, ref, az_s.at[q, 0, z_], az_r.at[q, 0, src], at(x, z_, core))
-
-    def gz_extra(v, r, q, e, z_):
-        ref = v.at[r, core, x, NZ + e]
-        return push(ref, ref, az_s.at[q, 1, z_], az_r.at[q, 1, e], at(x, z_, core))
-
-    def gather_z_start(v, r, q, value):
-        v[r, core, x, z] = value[:TILE]
-        over_z(lambda z_: gz_main(v, r, q, z, z_).start())
-
-        @pl.when(has_extra > 0)
-        def _():
-            v[r, core, x, NZ + which] = value[TILE:]
-            over_z(lambda z_: gz_extra(v, r, q, which, z_).start())
-
-        def drain():
-            over_z(lambda z_: gz_main(v, r, q, z, z_).wait_send())
-
-            @pl.when(has_extra > 0)
-            def _():
-                over_z(lambda z_: gz_extra(v, r, q, which, z_).wait_send())
-        drains.append(drain)
-
-    def gather_z_wait(v, r, q):
-        over_z(lambda z_: gz_main(v, r, q, z_, z_).wait_recv())
-        for e in range(extras):
-            @pl.when(z != extra_owner(e, core))
-            def _():
-                gz_extra(v, r, q, e, extra_owner(e, core)).wait_recv()
-
-    def g_core(v, r, q, c_, p):
-        ref = v.at[r, c_, p]
-        return push(ref, ref, ac_s.at[q, p], ac_r.at[q, p], sibling)
-
-    def g_x(v, r, q, p, dest):
+                received(v.at[r, core, x, 0], ae_r.at[q, e])
+
+    def to_sibling(v, r, q, p):
         ref = v.at[r, core, p]
-        return push(ref, ref, ax_s.at[q, dest], ax_r.at[q, p], at(dest, z, core))
+        push(ref, ref, ac_s.at[q], ac_r.at[q], sibling).start()
 
     def gather_x_start(v, r, q):
-        for d in hops4:
-            go(g_x(v, r, q, x, x_peer(d)))
-        go(g_core(v, r, q, core, x))
+        ref = v.at[r, core, x]
+        over_x(lambda x_: push(ref, ref, ax_s.at[q], ax_r.at[q, x], at(x_, z, core)).start())
+        sent(v.at[r, core, pl.ds(0, NX - 1)], ax_s.at[q])
+        to_sibling(v, r, q, x)
 
     def gather_x_forward(v, r, q):
         for d in (1, 3, 2):
             p = x_peer(d)
-            g_x(v, r, q, p, p).wait_recv()
-            go(g_core(v, r, q, core, p))
+            received(v.at[r, core, p], ax_r.at[q, p])
+            to_sibling(v, r, q, p)
+        sent(v.at[r, core], ac_s.at[q])
 
     def gather_core_wait(v, r, q):
-        for d in (0, 1, 3, 2):
-            g_core(v, r, q, 1 - core, wrap(x + d, NX)).wait_recv()
+        received(v.at[r, 1 - core], ac_r.at[q])
 
     def forward(r):
         value = vh[r].reshape(columns, 128)
         return jnp.dot(d_ref[...], value, preferred_element_type=F32) * mask_ref[...]
 
     def y_start(r, partial, norms):
-        yb[r, y] = partial
-        ny[r, y] = norms
+        yb[r, y, :half] = partial
+        yb[r, y, half:half + 8] = jnp.concatenate([norms, jnp.zeros((4, 128), F32)], axis=0)
         for d in hops4:
-            y_ = wrap(y + d, NY)
-            go(push(ny.at[r, y], ny.at[r, y], ny_s.at[r, y_], ny_r.at[r, y], y_peer(d)))
-            go(push(yb.at[r, y], yb.at[r, y], y_s.at[r, y_], y_r.at[r, y], y_peer(d)))
+            push(yb.at[r, y], yb.at[r, y], y_s.at[r], y_r.at[r], y_peer(d)).start()
+        sent(yb.at[r, pl.ds(0, NY - 1)], y_s.at[r])
 
     def y_wait(r):
-        for d in hops4:
-            y_ = wrap(y + d, NY)
-            push(ny.at[r, y], ny.at[r, y_], ny_s.at[r, y_], ny_r.at[r, y_], y_peer(d)).wait_recv()
-            push(yb.at[r, y], yb.at[r, y_], y_s.at[r, y_], y_r.at[r, y_], y_peer(d)).wait_recv()
-        return (
-            (yb[r, 0] + yb[r, 1]) + (yb[r, 2] + yb[r, 3]),
-            (ny[r, 0] + ny[r, 1]) + (ny[r, 2] + ny[r, 3]),
-        )
+        received(yb.at[r, pl.ds(0, NY - 1)], y_r.at[r])
+        value = (yb[r, 0] + yb[r, 1]) + (yb[r, 2] + yb[r, 3])
+        return value[:half], value[half:half + 4]
 
     def split(value):
         hi = value.astype(BF16)
@@ -353,9 +337,9 @@
         hi, lo = split(value)
         gather_z_start(vh, r, 2 * r, hi)
         n_z(k, norms)
-        gather_z_start(vl, r, 2 * r + 1, lo)
         gather_z_wait(vh, r, 2 * r)
         gather_x_start(vh, r, 2 * r)
+        gather_z_start(vl, r, 2 * r + 1, lo)
         n_x(k, n_z_sum(k))
         gather_x_forward(vh, r, 2 * r)
         n_core(k, n_x_sum(k))
@@ -458,23 +442,23 @@
         pltpu.VMEM((2, 2, TILE, 128), F32),
         pltpu.VMEM((2, NC, NX) + block, BF16),
         pltpu.VMEM((2, NC, NX) + block, BF16),
-        pltpu.VMEM((2, NY, rows // 2, 128), F32),
-        pltpu.VMEM((2, NY, 4, 128), F32),
+        pltpu.VMEM((2, NY, rows // 2 + 8, 128), F32),
         pltpu.VMEM((5, NC, 4, 128), F32),
         pltpu.VMEM((5, NX, 4, 128), F32),
         pltpu.VMEM((5, NZ, 4, 128), F32),
         dma((6,)),
-        dma((2, NX)), dma((2, NX)),
-        dma((2, NX)), dma((2, NX)),
-        dma((2, 2, NZ)), dma((2, 2, NZ)),
-        dma((4, 2, NZ)), dma((4, 2, NZ)),
-        dma((4, NX)), dma((4, NX)),
-        dma((4, NX)), dma((4, NX)),
-        dma((2, NY)), dma((2, NY)),
-        dma((2, NY)), dma((2, NY)),
+        dma((2,)), dma((2, NX)),
+        dma((2,)), dma((2,)),
+        dma((2,)), dma((2,)),
+        dma((2, tiles - NZ)), dma((2,)),
+        dma((4,)), dma((4,)),
+        dma((4,)), dma((4, tiles - NZ)),
+        dma((4,)), dma((4, NX)),
+        dma((4,)), dma((4,)),
+        dma((2,)), dma((2,)),
         dma((5,)), dma((5,)),
-        dma((5, NX)), dma((5, NX)),
-        dma((5, NZ)), dma((5, NZ)),
+        dma((5,)), dma((5,)),
+        dma((5,)), dma((5,)),
     ]
     return pl.pallas_call(
         kernel,

time: 123 us -> 115 us (0.935)
  Pallas kernels: 120 us -> 112 us
    pallas_call x1, Pallas kernels: 120 us -> 112 us  [body(): pl.pallas_call(kernel, out_shape=jax.ShapeDtypeStruct((columns, 128), F32...]
where the time goes in v3:
time: 115 us
  Pallas kernels  112 us (97%)
  local copies, waits for them, and re-layouts  2.41 us (2%)
    pallas_call x1, Pallas kernels, body(): pl.pallas_call(kernel, out_shape=jax.ShapeDtypeStruct((columns, 128), F32...  112 us
    unnamed x1, local copies, waits for them, and re-layouts  2.41 us

profile of v3, /device:TPU:1, one launch (start us, length us, event | category | flops | bytes accessed | tf_op | source)
XLA Modules:
  0.0 114.8 jit_solution(3141939424800227620)
XLA Ops:
  0.0 112.4 %shard_map.55 = f32[2432,128]{1,0:T(8,128)} custom-call(bf16[128,2432]{1,0:T(8,128)(2,1)} %design.1, bf16[64,128]{1,0:T(8,128)(2,1)} %bitcast.1, s32[1,4]{1,0:T(1,128)} %lengths.1, s32[1,4]{1,0:T(1,128)} %months.1, f32[2432]{0:T(1024)} %walk.1), custom_call_target="tpu_custom_call" | custom-call | tf_op jit(solution)/shard_map/pallas_call | solution.py:463
  112.4 2.4 %copy.7 = f32[2432,128]{1,0:T(8,128)} copy(f32[2432,128]{1,0:T(8,128)} %shard_map.55) | data formatting | bytes 2490368

commit v4 on v3

--- a/solution.py
+++ b/solution.py
@@ -12,6 +12,7 @@
 MESH = pl.DeviceIdType.MESH
 NX, NZ, NC, NY = 4, 16, 2, 4
 TILE = 16
+SPLIT = 10
 F32, BF16 = jnp.float32, jnp.bfloat16
 
 
@@ -28,6 +29,8 @@
     tiles = columns // (NC * NX * TILE)
     piece = tiles * TILE
     extras = tiles - NZ
+    halves = (pl.ds(0, SPLIT), pl.ds(SPLIT, tiles - SPLIT))
+    both = pl.ds(0, tiles)
     arc, y = lax.axis_index("arcs"), lax.axis_index("coef")
     core = lax.rem(arc, NC)
     z = lax.rem(arc // NC, NZ)
@@ -49,7 +52,7 @@
         return (arc, wrap(y + d, NY))
 
     def extra_owner(e, c_):
-        return 5 * e + 3 * c_
+        return 3 * e + c_
 
     drains = []
 
@@ -97,6 +100,7 @@
         hit = (z == extra_owner(e, core)).astype(jnp.int32)
         has_extra = has_extra + hit
         which = which + e * hit
+    late = (z >= SPLIT).astype(jnp.int32)
     base = (core * NX + x) * piece
     firsts = [base + z * TILE, base + (NZ + which) * TILE]
 
@@ -172,8 +176,6 @@
         if s == 1:
             keep = keep & (jnp.full((TILE, 128), has_extra, jnp.int32) > 0)
         keep_parts.append(keep.astype(F32))
-    w_own = jnp.concatenate(w_parts, axis=0)
-    keep_own = jnp.concatenate(keep_parts, axis=0)
 
     loads[3].wait()
     for j in range(columns // 128):
@@ -221,6 +223,7 @@
             push(cs.at[r, p], cr.at[r, p], cs_s.at[r], cs_r.at[r, p], sibling).start()
         loop(NX, theirs)
         sent(cs.at[r], cs_s.at[r])
+        n_x(k, n_core_sum(k))
 
         def mine(p):
             value = adjoint_piece(r, core, p)
@@ -229,56 +232,77 @@
 
         def away(p):
             xs[r, p] = mine(p)
-            push(xs.at[r, p], xr.at[r, x], xs_s.at[r], xs_r.at[r], at(p, z, core)).start()
+            half_away(p, 0)
+
+        def half_away(p, h):
+            push(xs.at[r, p, halves[h]], xr.at[r, x, halves[h]], xs_s.at[r], xs_r.at[r, h], at(p, z, core)).start()
         over_x(away)
+        over_x(lambda p: half_away(p, 1))
         sent(xs.at[r, pl.ds(0, NX - 1)], xs_s.at[r])
-        n_x(k, n_core_sum(k))
+        n_z(k, n_x_sum(k))
         xr[r, x] = mine(x)
-        n_z(k, n_x_sum(k))
-        received(xr.at[r, pl.ds(0, NX - 1)], xs_r.at[r])
-        tb[r] = (xr[r, 0] + xr[r, 1]) + (xr[r, 2] + xr[r, 3])
 
         def elsewhere(e, act):
             pl.when(z != extra_owner(e, core))(act)
 
-        for e in range(extras):
-            elsewhere(e, lambda e=e: push(
-                tb.at[r, NZ + e], zr.at[r, 1, z], ze_s.at[r, e], ze_r.at[r],
-                at(x, extra_owner(e, core), core)).start())
-        over_z(lambda z_: push(
-            tb.at[r, z_], zr.at[r, 0, z], zs_s.at[r], zs_r.at[r], at(x, z_, core)).start())
+        for h in range(2):
+            part = halves[h]
+            received(xr.at[r, pl.ds(0, NX - 1), part], xs_r.at[r, h])
+            tb[r, part] = (xr[r, 0, part] + xr[r, 1, part]) + (xr[r, 2, part] + xr[r, 3, part])
+            if h == 1:
+                for e in range(extras):
+                    elsewhere(e, lambda e=e: push(
+                        tb.at[r, NZ + e], zr.at[r, 1, z], ze_s.at[r, e], ze_r.at[r],
+                        at(x, extra_owner(e, core), core)).start())
+
+            def out_tile(z_, h=h):
+                @pl.when((z_ >= SPLIT) if h else (z_ < SPLIT))
+                def _():
+                    push(tb.at[r, z_], zr.at[r, 0, z], zs_s.at[r], zs_r.at[r], at(x, z_, core)).start()
+            over_z(out_tile)
         sent(tb.at[r, pl.ds(0, NZ - 1)], zs_s.at[r])
         zr[r, 0, z] = tb[r, z]
-        own[r, 1] = jnp.zeros((TILE, 128), F32)
-
-        @pl.when(has_extra > 0)
-        def _():
-            zr[r, 1, z] = tb[r, NZ + which]
-            received(zr.at[r, 1, pl.ds(0, NZ - 1)], ze_r.at[r])
-            own[r, 1] = jnp.sum(zr[r, 1], axis=0)
-        norm = n_z_sum(k)
-        received(zr.at[r, 0, pl.ds(0, NZ - 1)], zs_r.at[r])
-        own[r, 0] = jnp.sum(zr[r, 0], axis=0)
 
         def drain():
             for e in range(extras):
                 elsewhere(e, lambda e=e: push(
                     tb.at[r, 0], tb.at[r, 0], ze_s.at[r, e], ze_s.at[r, e], sibling).wait_send())
         drains.append(drain)
-        return own[r].reshape(2 * TILE, 128) * keep_own, norm
-
-    def gather_z_start(v, r, q, value):
+        return n_z_sum(k)
+
+    def owned(r, s):
+        if s == 0:
+            received(zr.at[r, 0, pl.ds(0, NZ - 1)], zs_r.at[r])
+            return jnp.sum(zr[r, 0], axis=0) * keep_parts[0]
+        own[r] = jnp.zeros((TILE, 128), F32)
+
+        @pl.when(has_extra > 0)
+        def _():
+            zr[r, 1, z] = tb[r, NZ + which]
+            received(zr.at[r, 1, pl.ds(0, NZ - 1)], ze_r.at[r])
+            own[r] = jnp.sum(zr[r, 1], axis=0)
+        return own[r] * keep_parts[1]
+
+    def keep_tile(v, r, s, value):
+        if s == 0:
+            v[r, core, x, z] = value
+        else:
+            @pl.when(has_extra > 0)
+            def _():
+                v[r, core, x, NZ + which] = value
+
+    def publish(v, r, q, s):
+        many = v.at[r, core, x, pl.ds(0, NZ - 1)]
+        if s == 0:
+            main = v.at[r, core, x, z]
+            over_z(lambda z_: push(main, main, az_s.at[q], az_r.at[q, late], at(x, z_, core)).start())
+            sent(many, az_s.at[q])
+            return
+
         @pl.when(has_extra > 0)
         def _():
             ref = v.at[r, core, x, NZ + which]
-            v[r, core, x, NZ + which] = value[TILE:]
             over_z(lambda z_: push(ref, ref, ae_s.at[q], ae_r.at[q, which], at(x, z_, core)).start())
-
-        main = v.at[r, core, x, z]
-        v[r, core, x, z] = value[:TILE]
-        over_z(lambda z_: push(main, main, az_s.at[q], az_r.at[q], at(x, z_, core)).start())
-        many = v.at[r, core, x, pl.ds(0, NZ - 1)]
-        sent(many, az_s.at[q])
 
         def drain():
             @pl.when(has_extra > 0)
@@ -286,32 +310,41 @@
                 push(many, many, ae_s.at[q], ae_s.at[q], sibling).wait_send()
         drains.append(drain)
 
-    def gather_z_wait(v, r, q):
-        received(v.at[r, core, x, pl.ds(0, NZ - 1)], az_r.at[q])
-        for e in range(extras):
-            @pl.when(z != extra_owner(e, core))
+    def tiles_wait(v, r, q, h):
+        count = NZ - SPLIT if h else SPLIT
+        for inside in range(2):
+            @pl.when(late == (h if inside else 1 - h))
             def _():
-                received(v.at[r, core, x, 0], ae_r.at[q, e])
-
-    def to_sibling(v, r, q, p):
-        ref = v.at[r, core, p]
+                received(v.at[r, core, x, pl.ds(0, count - inside)], az_r.at[q, h])
+        if h == 1:
+            for e in range(extras):
+                @pl.when(z != extra_owner(e, core))
+                def _():
+                    received(v.at[r, core, x, 0], ae_r.at[q, e])
+
+    def to_sibling(v, r, q, p, part):
+        ref = v.at[r, core, p, part]
         push(ref, ref, ac_s.at[q], ac_r.at[q], sibling).start()
 
-    def gather_x_start(v, r, q):
-        ref = v.at[r, core, x]
-        over_x(lambda x_: push(ref, ref, ax_s.at[q], ax_r.at[q, x], at(x_, z, core)).start())
-        sent(v.at[r, core, pl.ds(0, NX - 1)], ax_s.at[q])
-        to_sibling(v, r, q, x)
-
-    def gather_x_forward(v, r, q):
+    def gather_x_start(v, r, q, part, h):
+        ref = v.at[r, core, x, part]
+        over_x(lambda x_: push(ref, ref, ax_s.at[q], ax_r.at[q, h, x], at(x_, z, core)).start())
+        sent(v.at[r, core, pl.ds(0, NX - 1), part], ax_s.at[q])
+        to_sibling(v, r, q, x, part)
+
+    def gather_x_forward(v, r, q, part, h):
         for d in (1, 3, 2):
             p = x_peer(d)
-            received(v.at[r, core, p], ax_r.at[q, p])
-            to_sibling(v, r, q, p)
-        sent(v.at[r, core], ac_s.at[q])
+            received(v.at[r, core, p, part], ax_r.at[q, h, p])
+            to_sibling(v, r, q, p, part)
+        sent(v.at[r, core, pl.ds(0, NX), part], ac_s.at[q])
 
     def gather_core_wait(v, r, q):
         received(v.at[r, 1 - core], ac_r.at[q])
+
+    def rest_wait(r):
+        for h in range(2):
+            tiles_wait(vl, r, 2 * r + 1, h)
 
     def forward(r):
         value = vh[r].reshape(columns, 128)
@@ -333,53 +366,75 @@
         hi = value.astype(BF16)
         return hi, (value - hi.astype(F32)).astype(BF16)
 
-    def gather(r, k, value, norms):
-        hi, lo = split(value)
-        gather_z_start(vh, r, 2 * r, hi)
-        n_z(k, norms)
-        gather_z_wait(vh, r, 2 * r)
-        gather_x_start(vh, r, 2 * r)
-        gather_z_start(vl, r, 2 * r + 1, lo)
-        n_x(k, n_z_sum(k))
-        gather_x_forward(vh, r, 2 * r)
-        n_core(k, n_x_sum(k))
+    def gather(r, k, make, norms_of):
+        values = []
+        for s in range(2):
+            value = make(s, owned(r, s))
+            hi, lo = split(value)
+            keep_tile(vh, r, s, hi)
+            publish(vh, r, 2 * r, s)
+            keep_tile(vl, r, s, lo)
+            values.append(value)
+        n_z(k, norms_of(values))
+        for h in range(2):
+            tiles_wait(vh, r, 2 * r, h)
+            gather_x_start(vh, r, 2 * r, halves[h], h)
+            if h == 0:
+                n_x(k, n_z_sum(k))
+        for h in range(2):
+            gather_x_forward(vh, r, 2 * r, halves[h], h)
+            if h == 0:
+                n_core(k, n_x_sum(k))
+        for s in range(2):
+            publish(vl, r, 2 * r + 1, s)
         gather_core_wait(vh, r, 2 * r)
-        return n_core_sum(k)
+        return values, n_core_sum(k)
 
     def root(v):
         return jnp.sqrt(v + EPS)
 
-    def walk_of(v):
-        return w_own * (turn(v) - v)
-
-    got, norm = reduce_scatter(0, 0, padded([total(bc * bc)]))
+    def walk_of(s, v):
+        return w_parts[s] * (turn(v) - v)
+
+    def totals(parts):
+        return total(parts[0]) + total(parts[1])
+
+    norm = reduce_scatter(0, 0, padded([total(bc * bc)]))
     beta1 = root(fold(norm[0:1]))
-    v1 = got / beta1
-    dv = walk_of(v1)
-    dv8 = dv * 0.125
-    norms = gather(0, 1, v1, padded([total(v1 * v1), total(dv8 * dv8)]))
+
+    def norms1(v):
+        dv8 = [walk_of(s, v[s]) * 0.125 for s in range(2)]
+        return padded([totals([e * e for e in v]), totals([e * e for e in dv8])])
+
+    v1, norms = gather(0, 1, lambda s, got: got / beta1, norms1)
     y_start(0, compact(forward(0)), norms)
-    gather_z_wait(vl, 0, 1)
-    gather_x_start(vl, 0, 1)
     image, norms = y_wait(0)
 
     alpha1 = root(fold(norms[0:1]))
     o2 = image / alpha1 - alpha1 * (bc_ref[...] / beta1)
     u_ref[1] = expand(o2)
     walk2 = (norms[1:2] / (alpha1 * alpha1)) * 64.0
-    got, norm = reduce_scatter(1, 2, padded([total(o2 * o2)]))
+    norm = reduce_scatter(1, 2, padded([total(o2 * o2)]))
+    rest_wait(0)
+    gather_x_start(vl, 0, 1, both, 0)
     beta2 = jnp.sqrt(fold(norm[0:1]) + walk2 + EPS)
-    wz = (dv / alpha1) / beta2
-    v2 = got / beta2 - w_own * wz - beta2 * (v1 / alpha1)
-    dv8 = walk_of(v2) * 0.125
-    norms = gather(
-        1, 3, v2,
-        padded([total(v2 * v2), total(dv8 * dv8), total(dv8 * wz), total(wz * wz)]),
-    )
+    wz = [(walk_of(s, v1[s]) / alpha1) / beta2 for s in range(2)]
+
+    def second_vector(s, got):
+        return got / beta2 - w_parts[s] * wz[s] - beta2 * (v1[s] / alpha1)
+
+    def norms2(v):
+        dv8 = [walk_of(s, v[s]) * 0.125 for s in range(2)]
+        return padded([
+            totals([e * e for e in v]),
+            totals([e * e for e in dv8]),
+            totals([e * g for e, g in zip(dv8, wz)]),
+            totals([g * g for g in wz]),
+        ])
+
+    v2, norms = gather(1, 3, second_vector, norms2)
     y_start(1, compact(forward(1)), norms)
-    gather_z_wait(vl, 1, 3)
-    gather_x_start(vl, 1, 3)
-    gather_x_forward(vl, 0, 1)
+    gather_x_forward(vl, 0, 1, both, 0)
     image, norms = y_wait(1)
 
     alpha2 = root(fold(norms[0:1]))
@@ -389,8 +444,10 @@
     walk3 = (norms[1:2] / square) * 64.0 - 16.0 * norms[2:3] + square * norms[3:4]
     walk3 = jnp.maximum(walk3, 0.0)
     n_x(4, n_core_sum(4))
-    gather_x_forward(vl, 1, 3)
     n_z(4, n_x_sum(4))
+    rest_wait(1)
+    gather_x_start(vl, 1, 3, both, 0)
+    gather_x_forward(vl, 1, 3, both, 0)
     rho1 = jnp.sqrt(alpha1 * alpha1 + beta2 * beta2)
     cos1, sin1 = alpha1 / rho1, beta2 / rho1
     first_step = cos1 * beta1 / rho1
@@ -439,7 +496,7 @@
         pltpu.VMEM((2, NX) + block, F32),
         pltpu.VMEM((2,) + block, F32),
         pltpu.VMEM((2, 2, NZ, TILE, 128), F32),
-        pltpu.VMEM((2, 2, TILE, 128), F32),
+        pltpu.VMEM((2, TILE, 128), F32),
         pltpu.VMEM((2, NC, NX) + block, BF16),
         pltpu.VMEM((2, NC, NX) + block, BF16),
         pltpu.VMEM((2, NY, rows // 2 + 8, 128), F32),
@@ -448,12 +505,12 @@
         pltpu.VMEM((5, NZ, 4, 128), F32),
         dma((6,)),
         dma((2,)), dma((2, NX)),
-        dma((2,)), dma((2,)),
+        dma((2,)), dma((2, 2)),
         dma((2,)), dma((2,)),
         dma((2, tiles - NZ)), dma((2,)),
-        dma((4,)), dma((4,)),
+        dma((4,)), dma((4, 2)),
         dma((4,)), dma((4, tiles - NZ)),
-        dma((4,)), dma((4, NX)),
+        dma((4,)), dma((4, 2, NX)),
         dma((4,)), dma((4,)),
         dma((2,)), dma((2,)),
         dma((5,)), dma((5,)),

time: 115 us -> 108 us (0.939)
  Pallas kernels: 112 us -> 105 us
    pallas_call x1, Pallas kernels: 112 us -> 105 us  [body(): pl.pallas_call(kernel, out_shape=jax.ShapeDtypeStruct((columns, 128), F32...]
where the time goes in v4:
time: 108 us
  Pallas kernels  105 us (97%)
  local copies, waits for them, and re-layouts  2.41 us (2%)
    pallas_call x1, Pallas kernels, body(): pl.pallas_call(kernel, out_shape=jax.ShapeDtypeStruct((columns, 128), F32...  105 us
    unnamed x1, local copies, waits for them, and re-layouts  2.41 us

profile of v4, /device:TPU:1, one launch (start us, length us, event | category | flops | bytes accessed | tf_op | source)
XLA Modules:
  0.0 107.8 jit_solution(2314245969943970602)
XLA Ops:
  0.0 105.4 %shard_map.55 = f32[2432,128]{1,0:T(8,128)} custom-call(bf16[128,2432]{1,0:T(8,128)(2,1)} %design.1, bf16[64,128]{1,0:T(8,128)(2,1)} %bitcast.1, s32[1,4]{1,0:T(1,128)} %lengths.1, s32[1,4]{1,0:T(1,128)} %months.1, f32[2432]{0:T(1024)} %walk.1), custom_call_target="tpu_custom_call" | custom-call | tf_op jit(solution)/shard_map/pallas_call | solution.py:520
  105.4 2.4 %copy.7 = f32[2432,128]{1,0:T(8,128)} copy(f32[2432,128]{1,0:T(8,128)} %shard_map.55) | data formatting | bytes 2490368

commit v5 on v4

--- a/solution.py
+++ b/solution.py
@@ -19,10 +19,10 @@
 def kernel(
     design, observed, lengths, months, walk, out,
     d_ref, dt, ob_ref, len_ref, mon_ref, walk_ref, wt, mask_ref, u_ref, bc_ref,
-    cs, cr, xs, xr, tb, zr, own, vh, vl, yb, nc, nx, nz,
+    cs, cr, xs, xr, tb, zr, own, vh, vl, yb, ng, nz, d2, second,
     in_sem, cs_s, cs_r, xs_s, xs_r, zs_s, zs_r, ze_s, ze_r,
     az_s, az_r, ae_s, ae_r, ax_s, ax_r, ac_s, ac_r, y_s, y_r,
-    nc_s, nc_r, nx_s, nx_r, nz_s, nz_r,
+    ng_s, ng_r, nz_s, nz_r,
 ):
     rows = d_ref.shape[0]
     columns = d_ref.shape[1]
@@ -91,6 +91,7 @@
     over_z(lambda z_: greet(at(x, z_, core)))
     for d in hops4:
         greet(at(x_peer(d), z, core))
+        greet(at(x_peer(d), z, 1 - core))
         greet(y_peer(d))
     greet(sibling)
 
@@ -180,25 +181,33 @@
     loads[3].wait()
     for j in range(columns // 128):
         dt[j * 128:(j + 1) * 128, :] = d_ref[:, j * 128:(j + 1) * 128].T
-    pl.semaphore_wait(barrier, 1 + 2 * len(hops4) + NZ - 1)
-
-    def n_core(k, value):
-        nc[k, core] = value
-        push(nc.at[k, core], nc.at[k, core], nc_s.at[k], nc_r.at[k], sibling).start()
-        sent(nc.at[k, 0], nc_s.at[k])
-
-    def n_core_sum(k):
-        received(nc.at[k, 0], nc_r.at[k])
-        return nc[k, 0] + nc[k, 1]
-
-    def n_x(k, value):
-        nx[k, x] = value
-        over_x(lambda x_: push(nx.at[k, x], nx.at[k, x], nx_s.at[k], nx_r.at[k], at(x_, z, core)).start())
-        sent(nx.at[k, pl.ds(0, NX - 1)], nx_s.at[k])
-
-    def n_x_sum(k):
-        received(nx.at[k, pl.ds(0, NX - 1)], nx_r.at[k])
-        return (nx[k, 0] + nx[k, 1]) + (nx[k, 2] + nx[k, 3])
+    for c_ in range(NC):
+        d2[c_] = d_ref[:, c_ * (columns // NC):(c_ + 1) * (columns // NC)]
+
+    def adjoint_piece(r, h, p):
+        first = pl.multiple_of((h * NX + p) * piece, TILE)
+        value = jnp.dot(dt[pl.ds(first, piece), :], u_ref[r], preferred_element_type=F32)
+        return value.reshape(tiles, TILE, 128)
+
+    pl.semaphore_wait(barrier, 1 + 3 * len(hops4) + NZ - 1)
+
+    def n_group(k, value):
+        slot = x * NC + core
+        ng[k, slot] = value
+
+        def give(x_, c_):
+            push(ng.at[k, slot], ng.at[k, slot], ng_s.at[k], ng_r.at[k], at(x_, z, c_)).start()
+
+        def give_both(x_):
+            give(x_, core)
+            give(x_, 1 - core)
+        over_x(give_both)
+        give(x, 1 - core)
+        sent(ng.at[k, pl.ds(0, NX * NC - 1)], ng_s.at[k])
+
+    def n_group_sum(k):
+        received(ng.at[k, pl.ds(0, NX * NC - 1)], ng_r.at[k])
+        return jnp.sum(ng[k], axis=0)
 
     def n_z(k, value):
         nz[k, z] = value
@@ -209,13 +218,8 @@
         received(nz.at[k, pl.ds(0, NZ - 1)], nz_r.at[k])
         return jnp.sum(nz[k], axis=0)
 
-    def adjoint_piece(r, h, p):
-        first = pl.multiple_of((h * NX + p) * piece, TILE)
-        value = jnp.dot(dt[pl.ds(first, piece), :], u_ref[r], preferred_element_type=F32)
-        return value.reshape(tiles, TILE, 128)
-
     def reduce_scatter(r, k, norm_value):
-        n_core(k, norm_value)
+        n_group(k, norm_value)
 
         def theirs(i):
             p = wrap(x + nth(i, NX // 2), NX)
@@ -223,7 +227,6 @@
             push(cs.at[r, p], cr.at[r, p], cs_s.at[r], cs_r.at[r, p], sibling).start()
         loop(NX, theirs)
         sent(cs.at[r], cs_s.at[r])
-        n_x(k, n_core_sum(k))
 
         def mine(p):
             value = adjoint_piece(r, core, p)
@@ -239,7 +242,7 @@
         over_x(away)
         over_x(lambda p: half_away(p, 1))
         sent(xs.at[r, pl.ds(0, NX - 1)], xs_s.at[r])
-        n_z(k, n_x_sum(k))
+        n_z(k, n_group_sum(k))
         xr[r, x] = mine(x)
 
         def elsewhere(e, act):
@@ -346,9 +349,9 @@
         for h in range(2):
             tiles_wait(vl, r, 2 * r + 1, h)
 
-    def forward(r):
-        value = vh[r].reshape(columns, 128)
-        return jnp.dot(d_ref[...], value, preferred_element_type=F32) * mask_ref[...]
+    def forward(r, c_):
+        value = vh[r, c_].reshape(columns // NC, 128)
+        return jnp.dot(d2[c_], value, preferred_element_type=F32)
 
     def y_start(r, partial, norms):
         yb[r, y, :half] = partial
@@ -379,16 +382,18 @@
         for h in range(2):
             tiles_wait(vh, r, 2 * r, h)
             gather_x_start(vh, r, 2 * r, halves[h], h)
-            if h == 0:
-                n_x(k, n_z_sum(k))
+        n_group(k, n_z_sum(k))
+        for s in range(2):
+            publish(vl, r, 2 * r + 1, s)
         for h in range(2):
             gather_x_forward(vh, r, 2 * r, halves[h], h)
-            if h == 0:
-                n_core(k, n_x_sum(k))
-        for s in range(2):
-            publish(vl, r, 2 * r + 1, s)
+        image = forward(r, core)
         gather_core_wait(vh, r, 2 * r)
-        return values, n_core_sum(k)
+        image = image + forward(r, 1 - core)
+        y_start(r, compact(image * mask_ref[...]), n_group_sum(k))
+        rest_wait(r)
+        gather_x_start(vl, r, 2 * r + 1, both, 0)
+        return values
 
     def root(v):
         return jnp.sqrt(v + EPS)
@@ -406,8 +411,7 @@
         dv8 = [walk_of(s, v[s]) * 0.125 for s in range(2)]
         return padded([totals([e * e for e in v]), totals([e * e for e in dv8])])
 
-    v1, norms = gather(0, 1, lambda s, got: got / beta1, norms1)
-    y_start(0, compact(forward(0)), norms)
+    v1 = gather(0, 1, lambda s, got: got / beta1, norms1)
     image, norms = y_wait(0)
 
     alpha1 = root(fold(norms[0:1]))
@@ -415,8 +419,6 @@
     u_ref[1] = expand(o2)
     walk2 = (norms[1:2] / (alpha1 * alpha1)) * 64.0
     norm = reduce_scatter(1, 2, padded([total(o2 * o2)]))
-    rest_wait(0)
-    gather_x_start(vl, 0, 1, both, 0)
     beta2 = jnp.sqrt(fold(norm[0:1]) + walk2 + EPS)
     wz = [(walk_of(s, v1[s]) / alpha1) / beta2 for s in range(2)]
 
@@ -432,21 +434,17 @@
             totals([g * g for g in wz]),
         ])
 
-    v2, norms = gather(1, 3, second_vector, norms2)
-    y_start(1, compact(forward(1)), norms)
+    v2 = gather(1, 3, second_vector, norms2)
     gather_x_forward(vl, 0, 1, both, 0)
     image, norms = y_wait(1)
 
     alpha2 = root(fold(norms[0:1]))
     o3 = image / alpha2 - alpha2 * (o2 / beta2)
-    n_core(4, padded([total(o3 * o3)]))
+    n_group(4, padded([total(o3 * o3)]))
     square = alpha2 * alpha2
     walk3 = (norms[1:2] / square) * 64.0 - 16.0 * norms[2:3] + square * norms[3:4]
     walk3 = jnp.maximum(walk3, 0.0)
-    n_x(4, n_core_sum(4))
-    n_z(4, n_x_sum(4))
-    rest_wait(1)
-    gather_x_start(vl, 1, 3, both, 0)
+    n_z(4, n_group_sum(4))
     gather_x_forward(vl, 1, 3, both, 0)
     rho1 = jnp.sqrt(alpha1 * alpha1 + beta2 * beta2)
     cos1, sin1 = alpha1 / rho1, beta2 / rho1
@@ -456,17 +454,18 @@
     theta = sin1 * alpha2 / rho1
     gather_core_wait(vl, 0, 1)
     gather_core_wait(vl, 1, 3)
+    for c_ in range(NC):
+        for p in range(NX):
+            begin = (c_ * NX + p) * piece
+            for r, target in ((0, out), (1, second)):
+                value = vh[r, c_, p].astype(F32) + vl[r, c_, p].astype(F32)
+                target[begin:begin + piece, :] = value.reshape(piece, 128)
     beta3 = jnp.sqrt(fold(n_z_sum(4)[0:1]) + walk3 + EPS)
     rho2 = jnp.sqrt(rho_bar * rho_bar + beta3 * beta3)
     second_step = (rho_bar / rho2) * phi_bar / rho2
     weight1 = (first_step - second_step * theta) / alpha1
     weight2 = second_step / alpha2
-    for c_ in range(NC):
-        for p in range(NX):
-            first = (vh[0, c_, p].astype(F32) + vl[0, c_, p].astype(F32)).reshape(piece, 128)
-            second = (vh[1, c_, p].astype(F32) + vl[1, c_, p].astype(F32)).reshape(piece, 128)
-            begin = (c_ * NX + p) * piece
-            out[begin:begin + piece, :] = weight1 * first + weight2 * second
+    out[...] = weight1 * out[...] + weight2 * second[...]
 
     for drain in drains:
         drain()
@@ -500,9 +499,10 @@
         pltpu.VMEM((2, NC, NX) + block, BF16),
         pltpu.VMEM((2, NC, NX) + block, BF16),
         pltpu.VMEM((2, NY, rows // 2 + 8, 128), F32),
-        pltpu.VMEM((5, NC, 4, 128), F32),
-        pltpu.VMEM((5, NX, 4, 128), F32),
+        pltpu.VMEM((5, NX * NC, 4, 128), F32),
         pltpu.VMEM((5, NZ, 4, 128), F32),
+        pltpu.VMEM((NC, rows, columns // NC), BF16),
+        pltpu.VMEM((columns, 128), F32),
         dma((6,)),
         dma((2,)), dma((2, NX)),
         dma((2,)), dma((2, 2)),
@@ -513,7 +513,6 @@
         dma((4,)), dma((4, 2, NX)),
         dma((4,)), dma((4,)),
         dma((2,)), dma((2,)),
-        dma((5,)), dma((5,)),
         dma((5,)), dma((5,)),
         dma((5,)), dma((5,)),
     ]

time: 108 us -> 106 us (0.981)
    pallas_call x1, Pallas kernels: 105 us -> 104 us  [body(): pl.pallas_call(kernel, out_shape=jax.ShapeDtypeStruct((columns, 128), F32...]
where the time goes in v5:
time: 106 us
  Pallas kernels  104 us (98%)
  local copies, waits for them, and re-layouts  2.41 us (2%)
    pallas_call x1, Pallas kernels, body(): pl.pallas_call(kernel, out_shape=jax.ShapeDtypeStruct((columns, 128), F32...  104 us
    unnamed x1, local copies, waits for them, and re-layouts  2.41 us

profile of v5, /device:TPU:1, one launch (start us, length us, event | category | flops | bytes accessed | tf_op | source)
XLA Modules:
  0.0 106.3 jit_solution(2288467016070876038)
XLA Ops:
  0.0 103.8 %shard_map.55 = f32[2432,128]{1,0:T(8,128)} custom-call(bf16[128,2432]{1,0:T(8,128)(2,1)} %design.1, bf16[64,128]{1,0:T(8,128)(2,1)} %bitcast.1, s32[1,4]{1,0:T(1,128)} %lengths.1, s32[1,4]{1,0:T(1,128)} %months.1, f32[2432]{0:T(1024)} %walk.1), custom_call_target="tpu_custom_call" | custom-call | tf_op jit(solution)/shard_map/pallas_call | solution.py:519
  103.8 2.4 %copy.7 = f32[2432,128]{1,0:T(8,128)} copy(f32[2432,128]{1,0:T(8,128)} %shard_map.55) | data formatting | bytes 2490368

commit v6 on v5

--- a/solution.py
+++ b/solution.py
@@ -252,17 +252,17 @@
             part = halves[h]
             received(xr.at[r, pl.ds(0, NX - 1), part], xs_r.at[r, h])
             tb[r, part] = (xr[r, 0, part] + xr[r, 1, part]) + (xr[r, 2, part] + xr[r, 3, part])
+
+            def out_tile(z_, h=h):
+                @pl.when((z_ >= SPLIT) if h else (z_ < SPLIT))
+                def _():
+                    push(tb.at[r, z_], zr.at[r, 0, z], zs_s.at[r], zs_r.at[r], at(x, z_, core)).start()
+            over_z(out_tile)
             if h == 1:
                 for e in range(extras):
                     elsewhere(e, lambda e=e: push(
                         tb.at[r, NZ + e], zr.at[r, 1, z], ze_s.at[r, e], ze_r.at[r],
                         at(x, extra_owner(e, core), core)).start())
-
-            def out_tile(z_, h=h):
-                @pl.when((z_ >= SPLIT) if h else (z_ < SPLIT))
-                def _():
-                    push(tb.at[r, z_], zr.at[r, 0, z], zs_s.at[r], zs_r.at[r], at(x, z_, core)).start()
-            over_z(out_tile)
         sent(tb.at[r, pl.ds(0, NZ - 1)], zs_s.at[r])
         zr[r, 0, z] = tb[r, z]
 

time: 106 us -> 108 us (1.019)
    pallas_call x1, Pallas kernels: 104 us -> 105 us  [body(): pl.pallas_call(kernel, out_shape=jax.ShapeDtypeStruct((columns, 128), F32...]
where the time goes in v6:
time: 108 us
  Pallas kernels  105 us (97%)
  local copies, waits for them, and re-layouts  2.41 us (2%)
    pallas_call x1, Pallas kernels, body(): pl.pallas_call(kernel, out_shape=jax.ShapeDtypeStruct((columns, 128), F32...  105 us
    unnamed x1, local copies, waits for them, and re-layouts  2.41 us

profile of v6, /device:TPU:1, one launch (start us, length us, event | category | flops | bytes accessed | tf_op | source)
XLA Modules:
  0.0 107.7 jit_solution(9701114723093230547)
XLA Ops:
  0.0 105.3 %shard_map.55 = f32[2432,128]{1,0:T(8,128)} custom-call(bf16[128,2432]{1,0:T(8,128)(2,1)} %design.1, bf16[64,128]{1,0:T(8,128)(2,1)} %bitcast.1, s32[1,4]{1,0:T(1,128)} %lengths.1, s32[1,4]{1,0:T(1,128)} %months.1, f32[2432]{0:T(1024)} %walk.1), custom_call_target="tpu_custom_call" | custom-call | tf_op jit(solution)/shard_map/pallas_call | solution.py:519
  105.3 2.4 %copy.7 = f32[2432,128]{1,0:T(8,128)} copy(f32[2432,128]{1,0:T(8,128)} %shard_map.55) | data formatting | bytes 2490368

commit v7 on v5

--- a/solution.py
+++ b/solution.py
@@ -17,12 +17,12 @@
 
 
 def kernel(
-    design, observed, lengths, months, walk, out,
+    design, observed, lengths, months, walk, first_out, second_out, weight1_out, weight2_out,
     d_ref, dt, ob_ref, len_ref, mon_ref, walk_ref, wt, mask_ref, u_ref, bc_ref,
-    cs, cr, xs, xr, tb, zr, own, vh, vl, yb, ng, nz, d2, second,
+    cs, cr, xs, xr, tb, zr, own, vh, vl, yb, ng, nz, d2, joined,
     in_sem, cs_s, cs_r, xs_s, xs_r, zs_s, zs_r, ze_s, ze_r,
     az_s, az_r, ae_s, ae_r, ax_s, ax_r, ac_s, ac_r, y_s, y_r,
-    ng_s, ng_r, nz_s, nz_r,
+    ng_s, ng_r, nz_s, nz_r, out_s,
 ):
     rows = d_ref.shape[0]
     columns = d_ref.shape[1]
@@ -457,15 +457,24 @@
     for c_ in range(NC):
         for p in range(NX):
             begin = (c_ * NX + p) * piece
-            for r, target in ((0, out), (1, second)):
+            for r in range(2):
                 value = vh[r, c_, p].astype(F32) + vl[r, c_, p].astype(F32)
-                target[begin:begin + piece, :] = value.reshape(piece, 128)
+                joined[r, begin:begin + piece, :] = value.reshape(piece, 128)
+    stores = [
+        pltpu.make_async_copy(joined.at[r], target, out_s.at[r])
+        for r, target in enumerate((first_out, second_out))
+    ]
+    for store in stores:
+        store.start()
     beta3 = jnp.sqrt(fold(n_z_sum(4)[0:1]) + walk3 + EPS)
     rho2 = jnp.sqrt(rho_bar * rho_bar + beta3 * beta3)
     second_step = (rho_bar / rho2) * phi_bar / rho2
     weight1 = (first_step - second_step * theta) / alpha1
     weight2 = second_step / alpha2
-    out[...] = weight1 * out[...] + weight2 * second[...]
+    weight1_out[...] = weight1
+    weight2_out[...] = weight2
+    for store in stores:
+        store.wait()
 
     for drain in drains:
         drain()
@@ -502,7 +511,7 @@
         pltpu.VMEM((5, NX * NC, 4, 128), F32),
         pltpu.VMEM((5, NZ, 4, 128), F32),
         pltpu.VMEM((NC, rows, columns // NC), BF16),
-        pltpu.VMEM((columns, 128), F32),
+        pltpu.VMEM((2, columns, 128), F32),
         dma((6,)),
         dma((2,)), dma((2, NX)),
         dma((2,)), dma((2, 2)),
@@ -515,17 +524,21 @@
         dma((2,)), dma((2,)),
         dma((5,)), dma((5,)),
         dma((5,)), dma((5,)),
+        dma((2,)),
     ]
-    return pl.pallas_call(
+    vector = jax.ShapeDtypeStruct((columns, 128), F32)
+    weight = jax.ShapeDtypeStruct((1, 128), F32)
+    first, second, weight1, weight2 = pl.pallas_call(
         kernel,
-        out_shape=jax.ShapeDtypeStruct((columns, 128), F32),
+        out_shape=[vector, vector, weight, weight],
         in_specs=[hbm] * 5,
-        out_specs=vmem,
+        out_specs=[hbm, hbm, vmem, vmem],
         scratch_shapes=scratch,
         compiler_params=pltpu.CompilerParams(
             collective_id=0, has_side_effects=True, vmem_limit_bytes=63 * 1024 * 1024
         ),
     )(design, observed.T, arc_lengths, arc_months, walk_weight)
+    return weight1 * first + weight2 * second
 
 
 def solution(mesh):

time: 106 us -> 106 us (level)
  other arithmetic: 0 us -> 2.84 us
  local copies, waits for them, and re-layouts: 2.41 us -> 0 us
    add x0 -> x1, other arithmetic: none -> 2.84 us  [body(): return weight1 * first + weight2 * second]
    unnamed x1 -> x0, local copies, waits for them, and re-layouts: 2.41 us -> none
where the time goes in v7:
time: 106 us
  Pallas kernels  103 us (97%)
  other arithmetic  2.84 us (3%)
    pallas_call x1, Pallas kernels, body(): pl.pallas_call(kernel, out_shape=[vector, vector, weight, weight], in_spe...  103 us
    add x1, other arithmetic, body(): return weight1 * first + weight2 * second  2.84 us

profile of v7, /device:TPU:1, one launch (start us, length us, event | category | flops | bytes accessed | tf_op | source)
XLA Modules:
  0.0 105.9 jit_solution(5232223697578203909)
XLA Ops:
  0.0 103.1 %shard_map.55 = (f32[2432,128]{1,0:T(8,128)}, f32[2432,128]{1,0:T(8,128)}, f32[1,128]{1,0:T(1,128)}, f32[1,128]{1,0:T(1,128)}) custom-call(bf16[128,2432]{1,0:T(8,128)(2,1)} %design.1, bf16[64,128]{1,0:T(8,128)(2,1)} %bitcast.3, s32[1,4]{1,0:T(1,128)} %lengths.1, s32[1,4]{1,0:T(1,128)} %months.1, f32[2432]{0:T(1024)} %walk.1), custom_call_target="tpu_custom_call" | custom-call | tf_op jit(solution)/shard_map/pallas_call | solution.py:531
  103.1 2.8 %multiply_add_fusion = f32[2432,128]{1,0:T(8,128)} fusion(f32[2432,128]{1,0:T(8,128)} %get-tuple-element.12, f32[2432,128]{1,0:T(8,128)} %get-tuple-element.10, f32[128]{0:T(128)} %bitcast.5, f32[128]{0:T(128)} %bitcast.4), kind=kLoop, calls=%fused_computation | loop fusion | flops 933888 | bytes 3736576 | tf_op jit(solution)/shard_map/add | solution.py:541
